TPU v7x, 32 devices: a whole 2x2x4 slice. The times are simulated.
32 devices in a mesh: ctx: 16 (over z, y, x), heads: 2 (over core).
Axes of the slice: x: 2, y: 2, z: 4, core: 2. Of those that a mesh axis runs over, the one named last changes fastest.
Arguments:
- ssm_input: bfloat16 [3072, 8192], P('ctx', 'heads'), may hold values from -36 to 36
- gate_input: bfloat16 [3072, 8192], P('ctx', 'heads'), may hold values from -6 to 6
- write_proj: bfloat16 [3072, 128], P('ctx'), may hold values from -0.5 to 0.5
- read_proj: bfloat16 [3072, 128], P('ctx'), may hold values from -0.5 to 0.5
- log_decay: float32 [3072, 128], P('ctx', 'heads'), may hold values from -0.75 to 0, as said below
- skip_gain: float32 [128], P('heads'), may hold values from 0.5 to 2
- norm_gain: float32 [8192], P('heads'), may hold values from 0.1 to 1.9
- query_rows: bfloat16 [3072, 4096], P('ctx', 'heads'), may hold values from -6 to 6
- key_rows: bfloat16 [3072, 1024], P('ctx', 'heads'), may hold values from -6 to 6
- value_rows: bfloat16 [3072, 1024], P('ctx', 'heads'), may hold values from -6 to 6
Outputs:
- ssm_out: bfloat16 [3072, 8192], P('ctx', 'heads')
- attn_out: bfloat16 [3072, 4096], P('ctx', 'heads')
Inputs may be any that keep to these rules, and one draw needn't show every extreme that they name: `log_decay`: negative everywhere.
All inputs are finite; a program needn't handle non-finite values.
Results may differ from a plain program's by a relative error of at most 0.0075.
Values may be sent and summed in bfloat16 or wider, within the bound.
A program may use at most 128 MiB of HBM per device.

v0:
```python
import jax
import jax.numpy as jnp
from jax import lax
from jax.sharding import PartitionSpec as P

SSM_HEADS = 128
HEAD_P = 64
STATE = 128
QUERY_HEADS = 32
KV_HEADS = 8
HEAD_DIM = 128
SPAN = 64


def carried_in(part, axis, combine, identity):
    place = lax.axis_index(axis)
    gathered = jax.tree.map(lambda a: lax.all_gather(a, axis), part)
    state = jax.tree.map(lambda a, e: jnp.zeros_like(a) + jnp.asarray(e, a.dtype), part, identity)

    def one(step, state):
        return combine(
            state, jax.tree.map(lambda a: lax.dynamic_index_in_dim(a, step, 0, False), gathered)
        )

    return lax.fori_loop(0, place, one, state)


def chain_combine(earlier, later):
    return (earlier[0] * later[0], later[0][:, None, None] * earlier[1] + later[1])


def local_mixer(ssm_input, gate_input, write_proj, read_proj, log_decay, skip_gain, norm_gain):
    row_count, width_local = ssm_input.shape
    head_local = log_decay.shape[1]
    block_count = row_count // SPAN
    inputs_blk = ssm_input.reshape(block_count, SPAN, head_local, HEAD_P)
    inputs_float = inputs_blk.astype(jnp.float32)
    write_blk = write_proj.reshape(block_count, SPAN, STATE)
    read_blk = read_proj.reshape(block_count, SPAN, STATE)
    cum_decay = jnp.cumsum(log_decay.reshape(block_count, SPAN, head_local), axis=1)
    cum_heads = jnp.transpose(cum_decay, (0, 2, 1))
    causal = jnp.arange(SPAN)[:, None] >= jnp.arange(SPAN)[None, :]
    decay_gap = cum_heads[:, :, :, None] - cum_heads[:, :, None, :]
    decay_mask = jnp.where(causal, jnp.exp(jnp.where(causal, decay_gap, 0.0)), 0.0)
    intersection = jnp.einsum(
        "ctn,csn->cts", read_blk, write_blk, preferred_element_type=jnp.float32
    )
    mix_weights = intersection[:, None] * decay_mask
    y_local = jnp.einsum(
        "chts,cshp->cthp", mix_weights, inputs_float, precision=lax.Precision.HIGHEST
    )
    tail_decay = jnp.exp(cum_heads[:, :, -1:] - cum_heads)
    weighted_write = tail_decay[:, :, :, None] * write_blk[:, None].astype(jnp.float32)
    block_state = jnp.einsum(
        "cshp,chsn->chpn", inputs_float, weighted_write, precision=lax.Precision.HIGHEST
    )
    block_decay = jnp.exp(cum_heads[:, :, -1])

    def prefix_step(carry_in, block_item):
        return (chain_combine(carry_in, block_item), carry_in)

    start_pair = (
        jnp.ones((head_local,), jnp.float32),
        jnp.zeros((head_local, HEAD_P, STATE), jnp.float32),
    )
    device_pair, prefix_pair = lax.scan(prefix_step, start_pair, (block_decay, block_state))
    incoming = carried_in(device_pair, "ctx", chain_combine, start_pair)
    start_state = prefix_pair[0][:, :, None, None] * incoming[1][None] + prefix_pair[1]
    y_carry = (
        jnp.einsum(
            "ctn,chpn->cthp",
            read_blk.astype(jnp.float32),
            start_state,
            precision=lax.Precision.HIGHEST,
        )
        * jnp.exp(cum_decay)[:, :, :, None]
    )
    mixed_out = y_local + y_carry + skip_gain[None, None, :, None] * inputs_float
    gated = mixed_out.reshape(row_count, width_local) * jax.nn.silu(gate_input.astype(jnp.float32))
    square_total = lax.psum(jnp.sum(gated * gated, axis=1), "heads")
    row_scale = lax.rsqrt(square_total / (SSM_HEADS * HEAD_P) + 1e-05)
    return (gated * row_scale[:, None] * norm_gain[None, :]).astype(jnp.bfloat16)


def attend_block(
    state, query_block, query_positions, top_position, key_block, value_block, first_key
):
    scale_factor = 1.0 / HEAD_DIM**0.5
    key_count = key_block.shape[0]

    def compute(state_in):
        running_max, running_sum, running_acc = state_in
        scores = (
            jnp.einsum("gqd,ngd->gqn", query_block, key_block, preferred_element_type=jnp.float32)
            * scale_factor
        )
        key_positions = first_key + jnp.arange(key_count, dtype=jnp.int32)
        visible = key_positions[None, None, :] <= query_positions[None, :, None]
        block_max = jnp.max(jnp.where(visible, scores, -1e30), axis=2)
        new_max = jnp.maximum(running_max, block_max)
        weights = jnp.where(
            visible, jnp.exp(jnp.where(visible, scores - new_max[:, :, None], 0.0)), 0.0
        )
        rescale = jnp.exp(running_max - new_max)
        new_sum = rescale * running_sum + jnp.sum(weights, axis=2)
        new_acc = rescale[:, :, None] * running_acc + jnp.einsum(
            "gqn,ngd->gqd",
            weights.astype(jnp.bfloat16),
            value_block,
            preferred_element_type=jnp.float32,
        )
        return (new_max, new_sum, new_acc)

    return lax.cond(first_key > top_position, lambda state_in: state_in, compute, state)


def attention_local(query_rows, key_rows, value_rows):
    row_count = query_rows.shape[0]
    head_sets = key_rows.shape[1] // HEAD_DIM
    group_size = QUERY_HEADS // KV_HEADS
    own_index = lax.axis_index("ctx")
    query_stack = query_rows.reshape(row_count, head_sets, group_size, HEAD_DIM)
    query_stack = jnp.transpose(query_stack, (1, 0, 2, 3)).reshape(
        head_sets, row_count * group_size, HEAD_DIM
    )
    stacked_rows = jnp.arange(row_count * group_size, dtype=jnp.int32) // group_size
    own_positions = own_index * row_count + stacked_rows
    query_sets = [(query_stack, own_positions)]
    tops = [jnp.max(positions) for _, positions in query_sets]
    carries = tuple(
        (
            (
                jnp.full((head_sets, block.shape[1]), -1e30, jnp.float32),
                jnp.zeros((head_sets, block.shape[1]), jnp.float32),
                jnp.zeros((head_sets, block.shape[1], HEAD_DIM), jnp.float32),
            )
            for block, _ in query_sets
        )
    )
    key_piece = lax.all_gather(key_rows, "ctx", axis=0, tiled=True)
    value_piece = lax.all_gather(value_rows, "ctx", axis=0, tiled=True)
    piece_rows = key_piece.shape[0]
    key_blocks = key_piece.reshape(piece_rows // row_count, row_count, head_sets, HEAD_DIM)
    value_blocks = value_piece.reshape(piece_rows // row_count, row_count, head_sets, HEAD_DIM)
    offsets = row_count * jnp.arange(piece_rows // row_count, dtype=jnp.int32)

    def inner_step(states, block_item):
        key_block, value_block, first_key = block_item
        updated = tuple(
            (
                attend_block(
                    states[number],
                    query_sets[number][0],
                    query_sets[number][1],
                    tops[number],
                    key_block,
                    value_block,
                    first_key,
                )
                for number in range(len(query_sets))
            )
        )
        return (updated, None)

    result, _ = lax.scan(inner_step, carries, (key_blocks, value_blocks, offsets))
    finished = [(state[2] / state[1][:, :, None]).astype(jnp.bfloat16) for state in result]
    combined = finished[0]
    combined = combined.reshape(head_sets, row_count, group_size, HEAD_DIM)
    return jnp.transpose(combined, (1, 0, 2, 3)).reshape(
        row_count, head_sets * group_size * HEAD_DIM
    )


def body(
    ssm_input,
    gate_input,
    write_proj,
    read_proj,
    log_decay,
    skip_gain,
    norm_gain,
    query_rows,
    key_rows,
    value_rows,
):
    ssm_out = local_mixer(
        ssm_input, gate_input, write_proj, read_proj, log_decay, skip_gain, norm_gain
    )
    attn_out = attention_local(query_rows, key_rows, value_rows)
    return (ssm_out, attn_out)


def solution(mesh):
    in_specs = (
        P("ctx", "heads"),
        P("ctx", "heads"),
        P("ctx", None),
        P("ctx", None),
        P("ctx", "heads"),
        P("heads"),
        P("heads"),
        P("ctx", "heads"),
        P("ctx", "heads"),
        P("ctx", "heads"),
    )
    out_specs = (P("ctx", "heads"), P("ctx", "heads"))
    return jax.shard_map(body, mesh=mesh, in_specs=in_specs, out_specs=out_specs, check_vma=False)
```

profile of v0, /device:TPU:24, one launch (start us, length us, event | category | flops | bytes accessed | tf_op | source)
XLA Modules:
  0.0 564.3 jit_solution(17974713275050482958)
XLA Ops:
  10.0 5.5 reshape.102
  15.5 9.4 %fusion.53 = f32[3,64,64,128]{3,2,1,0:T(8,128)} fusion(f32[3,64,128]{2,1,0:T(8,128)S(1)} %convert_element_type.29, f32[3,64,64]{2,1,0:T(8,128)S(1)} %copy.39, bf16[3,64,64,64]{3,2,1,0:T(8,128)(2,1)} %reshape.102), kind=kOutput, calls=%fused_computation.73 | convolution fusion | flops 1209532416 | bytes 8011776 | tf_op jit(solution)/shard_map/cshp,chsn->chpn/dot_general | solution.py:54
  24.9 10.4 %while.46 = (s32[]{:T(128)}, f32[64]{0:T(128)S(1)}, f32[64,64,128]{2,1,0:T(8,128)S(1)}, f32[3,64]{1,0:T(4,128)S(1)}, f32[3,64,64,128]{3,2,1,0:T(8,128)}, /*index...) while((s32[]{:T(128)}, f32[64]{0:T(128)S(1)}, ...), condition=%wide.region_2.3_spmd.clone, body=%wide.region_1.2_spmd.clone.sunk | while | flops 2097283 | bytes 10488437 | solution.py:66
  38.7 34.2 %all-reduce = f32[1024]{0:T(1024)S(1)} all-reduce(f32[1024]{0:T(1024)S(1)} %dynamic-update-slice), channel_id=2, replica_groups=mesh['ctx'=16,'heads'=2] {'ctx'}, use_global_device_ids=true, to_apply=%add | all-reduce | flops 1024 | bytes 8192
  79.2 10.9 %fusion.34 = f32[3,64,64,64]{3,2,1,0:T(8,128)} fusion(f32[3,64,64]{2,1,0:T(8,128)S(1)} %copy.36, f32[3,64,64]{2,1,0:T(8,128)S(1)} %fusion.68, pred[64,64]{1,0:T(8,128)(4,1)S(1)} %iota_compare_fusion, bf16[3,64,64,64]{3,2,1,0:T(8,128)(2,1)S(1)} %copy-done.2), kind=kOutput, calls=%fused_computation.50 | convolution fusion | flops 607125504 | bytes 4820992 | tf_op jit(solution)/shard_map/chts,cshp->cthp/dot_general | solution.py:49
  96.4 52.0 %all-gather.8.cloned.1.call-done = bf16[3072,512]{1,0:T(8,128)(2,1)} async-done(((bf16[192,512]{1,0:T(8,128)(2,1)}), bf16[3072,512]{1,0:T(8,128)(2,1)}) %all-gather.8.cloned.1.call-update) | async-done | bytes 3145744 | tf_op jit(solution)/shard_map/all_gather | solution.py:141
  158.6 106.3 %while.45 = (s32[]{:T(128)}, f32[4,768]{1,0:T(4,128)S(1)}, f32[4,768]{1,0:T(4,128)S(1)}, f32[4,768,128]{2,1,0:T(8,128)S(1)}, s32[16]{0:T(128)S(1)}, /*index=5*/s...) while((s32[]{:T(128)}, f32[4,768]{1,0:T(4,128)S(1)}, ...), condition=%wide.region_13.14_spmd.clone, body=%wide.region_8.13_spmd.clone.sunk | while | flops 310604736 | bytes 12217147 | solution.py:165
  160.5 6.0 %conditional.3 = ((f32[4,768]{1,0:T(4,128)S(1)}, f32[4,768]{1,0:T(4,128)S(1)}, f32[4,768,128]{2,1,0:T(8,128)S(1)})) conditional(s32[]{:T(128)} %convert_element_type.58, (s32[]{:T(128)}, s32[]{:T(128)}, bf16[16,192,4,128]{3,1,2,0:T(8,128)(2,1)}, s32[]{:T(128)}, bf16[4,768,128]{2,1,0:T(8,128)(2,1)S(1)}, /*index=5*/f32[4,768]{1,0:T(4,128)S(1)}, ...), branch_computations={%region_9.11_spmd.clone, %region_12.12_spmd} | conditional | flops 310603968 | bytes 12210732 | solution.py:114
  168.3 5.8 %conditional.3 = ((f32[4,768]{1,0:T(4,128)S(1)}, f32[4,768]{1,0:T(4,128)S(1)}, f32[4,768,128]{2,1,0:T(8,128)S(1)})) conditional(s32[]{:T(128)} %convert_element_type.58, (s32[]{:T(128)}, s32[]{:T(128)}, bf16[16,192,4,128]{3,1,2,0:T(8,128)(2,1)}, s32[]{:T(128)}, bf16[4,768,128]{2,1,0:T(8,128)(2,1)S(1)}, /*index=5*/f32[4,768]{1,0:T(4,128)S(1)}, ...), branch_computations={%region_9.11_spmd.clone, %region_12.12_spmd} | conditional | flops 310603968 | bytes 12210732 | solution.py:114
  176.0 5.8 %conditional.3 = ((f32[4,768]{1,0:T(4,128)S(1)}, f32[4,768]{1,0:T(4,128)S(1)}, f32[4,768,128]{2,1,0:T(8,128)S(1)})) conditional(s32[]{:T(128)} %convert_element_type.58, (s32[]{:T(128)}, s32[]{:T(128)}, bf16[16,192,4,128]{3,1,2,0:T(8,128)(2,1)}, s32[]{:T(128)}, bf16[4,768,128]{2,1,0:T(8,128)(2,1)S(1)}, /*index=5*/f32[4,768]{1,0:T(4,128)S(1)}, ...), branch_computations={%region_9.11_spmd.clone, %region_12.12_spmd} | conditional | flops 310603968 | bytes 12210732 | solution.py:114
  183.8 5.8 %conditional.3 = ((f32[4,768]{1,0:T(4,128)S(1)}, f32[4,768]{1,0:T(4,128)S(1)}, f32[4,768,128]{2,1,0:T(8,128)S(1)})) conditional(s32[]{:T(128)} %convert_element_type.58, (s32[]{:T(128)}, s32[]{:T(128)}, bf16[16,192,4,128]{3,1,2,0:T(8,128)(2,1)}, s32[]{:T(128)}, bf16[4,768,128]{2,1,0:T(8,128)(2,1)S(1)}, /*index=5*/f32[4,768]{1,0:T(4,128)S(1)}, ...), branch_computations={%region_9.11_spmd.clone, %region_12.12_spmd} | conditional | flops 310603968 | bytes 12210732 | solution.py:114
  191.5 5.8 %conditional.3 = ((f32[4,768]{1,0:T(4,128)S(1)}, f32[4,768]{1,0:T(4,128)S(1)}, f32[4,768,128]{2,1,0:T(8,128)S(1)})) conditional(s32[]{:T(128)} %convert_element_type.58, (s32[]{:T(128)}, s32[]{:T(128)}, bf16[16,192,4,128]{3,1,2,0:T(8,128)(2,1)}, s32[]{:T(128)}, bf16[4,768,128]{2,1,0:T(8,128)(2,1)S(1)}, /*index=5*/f32[4,768]{1,0:T(4,128)S(1)}, ...), branch_computations={%region_9.11_spmd.clone, %region_12.12_spmd} | conditional | flops 310603968 | bytes 12210732 | solution.py:114
  199.2 5.8 %conditional.3 = ((f32[4,768]{1,0:T(4,128)S(1)}, f32[4,768]{1,0:T(4,128)S(1)}, f32[4,768,128]{2,1,0:T(8,128)S(1)})) conditional(s32[]{:T(128)} %convert_element_type.58, (s32[]{:T(128)}, s32[]{:T(128)}, bf16[16,192,4,128]{3,1,2,0:T(8,128)(2,1)}, s32[]{:T(128)}, bf16[4,768,128]{2,1,0:T(8,128)(2,1)S(1)}, /*index=5*/f32[4,768]{1,0:T(4,128)S(1)}, ...), branch_computations={%region_9.11_spmd.clone, %region_12.12_spmd} | conditional | flops 310603968 | bytes 12210732 | solution.py:114
  206.9 5.8 %conditional.3 = ((f32[4,768]{1,0:T(4,128)S(1)}, f32[4,768]{1,0:T(4,128)S(1)}, f32[4,768,128]{2,1,0:T(8,128)S(1)})) conditional(s32[]{:T(128)} %convert_element_type.58, (s32[]{:T(128)}, s32[]{:T(128)}, bf16[16,192,4,128]{3,1,2,0:T(8,128)(2,1)}, s32[]{:T(128)}, bf16[4,768,128]{2,1,0:T(8,128)(2,1)S(1)}, /*index=5*/f32[4,768]{1,0:T(4,128)S(1)}, ...), branch_computations={%region_9.11_spmd.clone, %region_12.12_spmd} | conditional | flops 310603968 | bytes 12210732 | solution.py:114
  214.7 5.9 %conditional.3 = ((f32[4,768]{1,0:T(4,128)S(1)}, f32[4,768]{1,0:T(4,128)S(1)}, f32[4,768,128]{2,1,0:T(8,128)S(1)})) conditional(s32[]{:T(128)} %convert_element_type.58, (s32[]{:T(128)}, s32[]{:T(128)}, bf16[16,192,4,128]{3,1,2,0:T(8,128)(2,1)}, s32[]{:T(128)}, bf16[4,768,128]{2,1,0:T(8,128)(2,1)S(1)}, /*index=5*/f32[4,768]{1,0:T(4,128)S(1)}, ...), branch_computations={%region_9.11_spmd.clone, %region_12.12_spmd} | conditional | flops 310603968 | bytes 12210732 | solution.py:114
  222.4 5.8 %conditional.3 = ((f32[4,768]{1,0:T(4,128)S(1)}, f32[4,768]{1,0:T(4,128)S(1)}, f32[4,768,128]{2,1,0:T(8,128)S(1)})) conditional(s32[]{:T(128)} %convert_element_type.58, (s32[]{:T(128)}, s32[]{:T(128)}, bf16[16,192,4,128]{3,1,2,0:T(8,128)(2,1)}, s32[]{:T(128)}, bf16[4,768,128]{2,1,0:T(8,128)(2,1)S(1)}, /*index=5*/f32[4,768]{1,0:T(4,128)S(1)}, ...), branch_computations={%region_9.11_spmd.clone, %region_12.12_spmd} | conditional | flops 310603968 | bytes 12210732 | solution.py:114
  230.2 5.8 %conditional.3 = ((f32[4,768]{1,0:T(4,128)S(1)}, f32[4,768]{1,0:T(4,128)S(1)}, f32[4,768,128]{2,1,0:T(8,128)S(1)})) conditional(s32[]{:T(128)} %convert_element_type.58, (s32[]{:T(128)}, s32[]{:T(128)}, bf16[16,192,4,128]{3,1,2,0:T(8,128)(2,1)}, s32[]{:T(128)}, bf16[4,768,128]{2,1,0:T(8,128)(2,1)S(1)}, /*index=5*/f32[4,768]{1,0:T(4,128)S(1)}, ...), branch_computations={%region_9.11_spmd.clone, %region_12.12_spmd} | conditional | flops 310603968 | bytes 12210732 | solution.py:114
  237.9 5.8 %conditional.3 = ((f32[4,768]{1,0:T(4,128)S(1)}, f32[4,768]{1,0:T(4,128)S(1)}, f32[4,768,128]{2,1,0:T(8,128)S(1)})) conditional(s32[]{:T(128)} %convert_element_type.58, (s32[]{:T(128)}, s32[]{:T(128)}, bf16[16,192,4,128]{3,1,2,0:T(8,128)(2,1)}, s32[]{:T(128)}, bf16[4,768,128]{2,1,0:T(8,128)(2,1)S(1)}, /*index=5*/f32[4,768]{1,0:T(4,128)S(1)}, ...), branch_computations={%region_9.11_spmd.clone, %region_12.12_spmd} | conditional | flops 310603968 | bytes 12210732 | solution.py:114
  245.6 5.8 %conditional.3 = ((f32[4,768]{1,0:T(4,128)S(1)}, f32[4,768]{1,0:T(4,128)S(1)}, f32[4,768,128]{2,1,0:T(8,128)S(1)})) conditional(s32[]{:T(128)} %convert_element_type.58, (s32[]{:T(128)}, s32[]{:T(128)}, bf16[16,192,4,128]{3,1,2,0:T(8,128)(2,1)}, s32[]{:T(128)}, bf16[4,768,128]{2,1,0:T(8,128)(2,1)S(1)}, /*index=5*/f32[4,768]{1,0:T(4,128)S(1)}, ...), branch_computations={%region_9.11_spmd.clone, %region_12.12_spmd} | conditional | flops 310603968 | bytes 12210732 | solution.py:114
  253.3 5.8 %conditional.3 = ((f32[4,768]{1,0:T(4,128)S(1)}, f32[4,768]{1,0:T(4,128)S(1)}, f32[4,768,128]{2,1,0:T(8,128)S(1)})) conditional(s32[]{:T(128)} %convert_element_type.58, (s32[]{:T(128)}, s32[]{:T(128)}, bf16[16,192,4,128]{3,1,2,0:T(8,128)(2,1)}, s32[]{:T(128)}, bf16[4,768,128]{2,1,0:T(8,128)(2,1)S(1)}, /*index=5*/f32[4,768]{1,0:T(4,128)S(1)}, ...), branch_computations={%region_9.11_spmd.clone, %region_12.12_spmd} | conditional | flops 310603968 | bytes 12210732 | solution.py:114
  267.1 233.1 %all-gather.10.cloned.1.call-done = f32[1024,64,128]{2,1,0:T(8,128)} async-done(((f32[64,64,128]{2,1,0:T(8,128)}), f32[1024,64,128]{2,1,0:T(8,128)}) %all-gather.10.cloned.1.call-update) | async-done | bytes 33554448 | tf_op jit(solution)/shard_map/all_gather | solution.py:17
  500.4 24.5 %while.44 = (s32[]{:T(128)}, f32[64,64,128]{2,1,0:T(8,128)S(1)}, s32[]{:T(128)}, f32[16,64]{1,0:T(8,128)S(1)}, f32[16,64,64,128]{3,2,1,0:T(8,128)}, /*index=5*/s32[]{:T(128)}, s32[]{:T(128)}, s32[]{:T(128)}) while((s32[]{:T(128)}, f32[64,64,128]{2,1,0:T(8,128)S(1)}, s32[]{:T(128)}, f32[16,64]{1,0:T(8,128)S(1)}, f32[16,64,64,128]{3,2,1,0:T(8,128)}, ...), condition=%wide.region_4.5_spmd, body=%wide.region_3.4_spmd.sunk | while | flops 1048581 | bytes 6292351 | solution.py:25
  525.0 13.2 %fusion.28 = f32[3,64,64,64]{3,1,2,0:T(8,128)S(1)} fusion(f32[3,64,64,64]{3,2,1,0:T(8,128)} %fusion.34, f32[64]{0:T(128)S(1)} %copy-done.6, f32[3,64,64]{1,2,0:T(8,128)S(1)} %copy.42, bf16[3,64,128,1]{2,1,3,0:T(8,128)(2,1)S(1)} %bitcast.91, f32[3,64,64,128]{3,2,1,0:T(8,128)} %get-tuple-element.226, f32[64,64,128]{2,1,0:T(8,128)S(1)} %get-tuple-element.225, ...), kind=kOutput, calls=%fused_computation.44 | convolution fusion | flops 1215037440 | bytes 16352256 | tf_op jit(solution)/shard_map/ctn,chpn->cthp/dot_general | solution.py:70
  538.2 6.3 %copy.44 = f32[3,64,64,64]{3,2,1,0:T(8,128)} copy(f32[3,64,64,64]{3,1,2,0:T(8,128)S(1)} %fusion.28) | data formatting | bytes 6291456 | tf_op jit(solution)/shard_map/add | solution.py:78
  (268 shorter events, 162.1 us)
Async XLA Ops:
  7.2 71.9 %copy-start = (bf16[192,128]{1,0:T(8,128)(2,1)S(1)}, bf16[192,128]{1,0:T(8,128)(2,1)}, u32[]{:S(2)}) copy-start(bf16[192,128]{1,0:T(8,128)(2,1)} %param.21) | copy-start | bytes 147460
  7.2 8.3 %copy-start.4 = (bf16[192,128]{1,0:T(8,128)(2,1)S(1)}, bf16[192,128]{1,0:T(8,128)(2,1)}, u32[]{:S(2)}) copy-start(bf16[192,128]{1,0:T(8,128)(2,1)} %param.20) | copy-start | bytes 147460
  7.2 82.9 %all-gather.6.cloned.1.call-start = ((), (), s32[]{:S(2)}) async-start(), calls=%async_computation | async-start | bytes 3342336 | tf_op jit(solution)/shard_map/all_gather | solution.py:140
  7.9 140.5 %all-gather.8.cloned.1.call-start = ((), (), s32[]{:S(2)}) async-start(), calls=%async_computation.1 | async-start | bytes 3342336 | tf_op jit(solution)/shard_map/all_gather | solution.py:141
  8.7 491.5 %all-gather.10.cloned.1.call-start = ((), (), s32[]{:S(2)}) async-start(), calls=%async_computation.2 | async-start | bytes 35651584 | tf_op jit(solution)/shard_map/all_gather | solution.py:17
  24.9 11.9 %copy-start.7 = (u32[32]{0:T(128)S(1)}, u32[32]{0:T(128)}, u32[]{:S(2)}) copy-start(u32[32]{0:T(128)} %constant.111) | copy-start | bytes 388
  35.3 1.3 copy-start.1
  36.7 42.5 %copy-start.2 = (bf16[3,64,64,64]{3,2,1,0:T(8,128)(2,1)S(1)}, bf16[3,64,64,64]{3,2,1,0:T(8,128)(2,1)}, u32[]{:S(2)}) copy-start(bf16[3,64,64,64]{3,2,1,0:T(8,128)(2,1)} %reshape.102) | copy-start | bytes 4718596
  154.0 4.6 copy-start.3
  500.4 24.5 %copy-start.6 = (f32[64]{0:T(128)S(1)}, f32[64]{0:T(128)}, u32[]{:S(2)}) copy-start(f32[64]{0:T(128)} %param.23) | copy-start | bytes 772
  549.0 5.1 copy-start.5
Sparse Core Ops, SparseCore 0:
  10.8 68.0 all-gather.5
  81.7 66.7 all-gather.7
  151.2 348.9 all-gather.9
where the time goes:
time: 572 us; the launch traced here: 564 us
  waiting for transfers between devices  286 us (50%)
  matrix products  90 us (16%)
  other arithmetic  60.3 us (11%)
  local copies, waits for them, and re-layouts  53.2 us (9%)
  blocking collectives  36.7 us (6%)
  loops' own time  22.5 us (4%)
  between operations  15.1 us (3%)
    all_gather x1, waiting for transfers between devices, carried_in(): gathered = jax.tree.map(lambda a: lax.all_gather(a, axis), part)  233 us
    all_gather x1, waiting for transfers between devices, attention_local(): value_piece = lax.all_gather(value_rows, 'ctx', axis=0, tiled=True)  52 us
    dot_general x13, matrix products, compute(): jnp.einsum('gqn,ngd->gqd', weights.astype(jnp.bfloat16), value_block, pre...  36.7 us
    unnamed x1, blocking collectives  34.2 us
    add x15, other arithmetic, chain_combine(): later[0][:, None, None] * earlier[1] + later[1]  29.4 us
    another operation x1, loops' own time, attention_local(): lax.scan(inner_step, carries, (key_blocks, value_blocks, offsets))  20.8 us
    dot_general x13, matrix products, compute(): jnp.einsum('gqd,ngd->gqn', query_block, key_block, preferred_element_type...  19.6 us
    dot_general x1, matrix products, local_mixer(): jnp.einsum('ctn,chpn->cthp', read_blk.astype(jnp.float32), start_state, p...  13.2 us
  transfers between devices with their start and end apart: 3, of which 2 were waited for; matrix products, arithmetic and copies ran while one was open for 26% of the time, Pallas kernels for 0%

commit v1 on v0

--- a/solution.py
+++ b/solution.py
@@ -1,6 +1,11 @@
+import functools
+import math
+
 import jax
 import jax.numpy as jnp
 from jax import lax
+from jax.experimental import pallas as pl
+from jax.experimental.pallas import tpu as pltpu
 from jax.sharding import PartitionSpec as P
 
 SSM_HEADS = 128
@@ -190,6 +195,318 @@
     return (ssm_out, attn_out)
 
 
+GROUP = 4
+WIDE = 8
+F32 = jnp.float32
+BF16 = jnp.bfloat16
+LOG2E = math.log2(math.e)
+
+
+def expand_heads(per_head):
+    shape = (WIDE, WIDE * HEAD_P)
+    first = lax.broadcasted_iota(jnp.int32, shape, 0) * HEAD_P
+    column = lax.broadcasted_iota(jnp.int32, shape, 1)
+    spread = jnp.where((column >= first) & (column < first + HEAD_P), 1.0, 0.0).astype(BF16)
+    high = per_head.astype(BF16)
+    low = (per_head - high.astype(F32)).astype(BF16)
+    return jnp.dot(high, spread, preferred_element_type=F32) + jnp.dot(
+        low, spread, preferred_element_type=F32
+    )
+
+
+def state_kernel(x_ref, write_ref, cum_ref, out_ref):
+    cum = cum_ref[0]
+    rows = cum.shape[0]
+    weight = expand_heads(jnp.exp(cum[rows - 1 :, :] - cum))
+    scaled = (x_ref[...].astype(F32) * weight).astype(BF16)
+    out_ref[...] = lax.dot_general(
+        scaled, write_ref[...], (((0,), (0,)), ((), ())), preferred_element_type=F32
+    ).astype(BF16)
+
+
+def local_kernel(x_ref, write_ref, read_ref, cum_ref, cum_t_ref, skip_ref, out_ref):
+    rows = x_ref.shape[0]
+    inner = lax.dot_general(
+        read_ref[...], write_ref[...], (((1,), (1,)), ((), ())), preferred_element_type=F32
+    )
+    later = lax.broadcasted_iota(jnp.int32, (rows, rows), 0)
+    earlier = lax.broadcasted_iota(jnp.int32, (rows, rows), 1)
+    inner = jnp.where(earlier <= later, inner, 0.0)
+    cum = cum_ref[0]
+    cum_t = cum_t_ref[...]
+    left = lax.broadcasted_iota(jnp.int32, (rows, 2 * HEAD_P), 1) < HEAD_P
+    for pair in range(WIDE // 2):
+        columns = slice(pair * 2 * HEAD_P, (pair + 1) * 2 * HEAD_P)
+        x_pair = x_ref[:, columns]
+        halves = []
+        for h in (2 * pair, 2 * pair + 1):
+            gap = cum[:, h : h + 1] - cum_t[h : h + 1, :]
+            mix = (jnp.exp(jnp.minimum(gap, 0.0)) * inner).astype(BF16)
+            halves.append(jnp.dot(mix, x_pair, preferred_element_type=F32))
+        mixed = jnp.where(left, halves[0], halves[1])
+        out_ref[:, columns] = mixed + skip_ref[:, columns] * x_pair.astype(F32)
+
+
+def gate_kernel(part_ref, gate_ref, read_ref, cum_ref, start_ref, out_ref, square_ref):
+    carry = lax.dot_general(
+        read_ref[...], start_ref[...], (((1,), (1,)), ((), ())), preferred_element_type=F32
+    )
+    gate = gate_ref[...].astype(F32)
+    mixed = part_ref[...] + expand_heads(jnp.exp(cum_ref[0])) * carry
+    gated = mixed * (gate / (1.0 + jnp.exp(-gate)))
+    out_ref[...] = gated
+    square = gated * gated
+    total = square[:, :128]
+    for k in range(1, square.shape[1] // 128):
+        total = total + square[:, k * 128 : (k + 1) * 128]
+
+    @pl.when(pl.program_id(0) == 0)
+    def _():
+        square_ref[...] = total
+
+    @pl.when(pl.program_id(0) > 0)
+    def _():
+        square_ref[...] += total
+
+
+def attend_kernel(rows, first, last, *refs):
+    info_ref, q_ref, kv_ref = refs[:3]
+    state_in = refs[3 : 3 + (0 if first else 3)]
+    outs = refs[3 + len(state_in) :]
+    factor = LOG2E / math.sqrt(HEAD_DIM)
+    heads = q_ref.shape[2] // HEAD_DIM
+    key_count = GROUP * rows
+    block = pl.program_id(0)
+    place = info_ref[0]
+
+    def finish(h, new_max, new_sum, new_acc):
+        if last:
+            total = jnp.sum(new_sum, axis=1, keepdims=True)
+            outs[0][0, :, h * HEAD_DIM : (h + 1) * HEAD_DIM] = (new_acc / total).astype(BF16)
+        else:
+            outs[0][0, h] = jnp.broadcast_to(new_max, (rows, HEAD_DIM))
+            outs[1][0, h] = new_sum
+            outs[2][0, h] = new_acc
+
+    def compute():
+        keys = kv_ref[:, :, :HEAD_DIM].reshape(key_count, HEAD_DIM)
+        values = kv_ref[:, :, HEAD_DIM:].reshape(key_count, HEAD_DIM)
+        if first:
+            column = lax.broadcasted_iota(jnp.int32, (1, key_count), 1)
+            shift = (place - 0) * rows
+            for j in range(1, GROUP):
+                shift = jnp.where(column >= j * rows, ((place ^ j) - j) * rows, shift)
+            row = lax.broadcasted_iota(jnp.int32, (rows, 1), 0) + (place ^ block) * rows
+            visible = column + shift <= row
+        for h in range(heads):
+            query = q_ref[0, :, h * HEAD_DIM : (h + 1) * HEAD_DIM]
+            scores = lax.dot_general(
+                query, keys, (((1,), (1,)), ((), ())), preferred_element_type=F32
+            )
+            if first:
+                scores = jnp.where(visible, scores, -1e30)
+            new_max = jnp.max(scores, axis=1, keepdims=True)
+            if not first:
+                new_max = jnp.maximum(new_max, state_in[0][0, h][:, :1])
+            weights = jnp.exp2((scores - new_max) * factor)
+            new_sum = weights[:, :HEAD_DIM]
+            for k in range(1, key_count // HEAD_DIM):
+                new_sum = new_sum + weights[:, k * HEAD_DIM : (k + 1) * HEAD_DIM]
+            new_acc = jnp.dot(weights.astype(BF16), values, preferred_element_type=F32)
+            if not first:
+                rescale = jnp.exp2((state_in[0][0, h] - new_max) * factor)
+                new_sum = new_sum + rescale * state_in[1][0, h]
+                new_acc = new_acc + rescale * state_in[2][0, h]
+            finish(h, new_max, new_sum, new_acc)
+
+    if first:
+        compute()
+    else:
+        seen = info_ref[1] > 0
+        pl.when(seen)(compute)
+
+        @pl.when(jnp.logical_not(seen))
+        def _():
+            for h in range(heads):
+                finish(h, state_in[0][0, h][:, :1], state_in[1][0, h], state_in[2][0, h])
+
+
+def attend_step(info, query, keys_values, state, last):
+    first = state is None
+    rows, width = query.shape[1:]
+    heads = width // HEAD_DIM
+    state_shape = jax.ShapeDtypeStruct((GROUP, heads, rows, HEAD_DIM), F32)
+    state_spec = pl.BlockSpec((1, heads, rows, HEAD_DIM), lambda i: (i, 0, 0, 0))
+    query_spec = pl.BlockSpec((1, rows, width), lambda i: (i, 0, 0))
+    return pl.pallas_call(
+        functools.partial(attend_kernel, rows, first, last),
+        grid=(GROUP,),
+        in_specs=[
+            pl.BlockSpec(memory_space=pltpu.SMEM),
+            query_spec,
+            pl.BlockSpec(keys_values.shape, lambda i: (0, 0, 0)),
+        ]
+        + ([] if first else [state_spec] * 3),
+        out_specs=query_spec if last else [state_spec] * 3,
+        out_shape=jax.ShapeDtypeStruct(query.shape, BF16) if last else [state_shape] * 3,
+        compiler_params=pltpu.CompilerParams(vmem_limit_bytes=40 * 2**20),
+        cost_estimate=pl.CostEstimate(
+            flops=4 * GROUP * heads * rows * GROUP * rows * HEAD_DIM,
+            bytes_accessed=12 * 2**20,
+            transcendentals=GROUP * heads * rows * GROUP * rows,
+        ),
+        name="attend",
+    )(info, query, keys_values, *(() if first else state))
+
+
+def grouped_body(
+    ctx_size,
+    ssm_input,
+    gate_input,
+    write_proj,
+    read_proj,
+    log_decay,
+    skip_gain,
+    norm_gain,
+    query_rows,
+    key_rows,
+    value_rows,
+):
+    rows, width = ssm_input.shape
+    head_local = log_decay.shape[1]
+    steps = head_local // WIDE
+    block = WIDE * HEAD_P
+    groups = ctx_size // GROUP
+    own = lax.axis_index("ctx")
+    place = lax.rem(own, GROUP)
+    level = lax.div(own, GROUP)
+
+    def swap(piece, j):
+        return lax.ppermute(piece, "ctx", [(i, i ^ j) for i in range(ctx_size)])
+
+    def upward(piece):
+        pairs = [(i, i + GROUP) for i in range(ctx_size - GROUP)]
+        return jax.tree.map(lambda a: lax.ppermute(a, "ctx", pairs), piece)
+
+    def pick(pieces, index):
+        return lax.dynamic_index_in_dim(pieces, index, 0, False)
+
+    def trade(pick_for):
+        return [
+            pick_for(place ^ j) if j == 0 else swap(pick_for(place ^ j), j) for j in range(GROUP)
+        ]
+
+    key_sets = key_rows.shape[1] // GROUP
+    query_sets = query_rows.shape[1] // GROUP
+
+    def part_of(array, size, index):
+        return lax.dynamic_slice_in_dim(array, index * size, size, 1)
+
+    keys_values = jnp.stack(
+        trade(
+            lambda p: jnp.concatenate(
+                [part_of(key_rows, key_sets, p), part_of(value_rows, key_sets, p)], axis=1
+            )
+        )
+    )
+    query = jnp.stack(trade(lambda p: part_of(query_rows, query_sets, p)))
+
+    causal = (jnp.arange(rows)[:, None] >= jnp.arange(rows)[None, :]).astype(F32)
+    cum = jnp.dot(causal, log_decay, precision=lax.Precision.HIGHEST)
+    cum_blocks = jnp.transpose(cum.reshape(rows, steps, WIDE), (1, 0, 2))
+    cum_t = cum.T
+    x_spec = pl.BlockSpec((rows, block), lambda i: (0, i))
+    proj_spec = pl.BlockSpec((rows, STATE), lambda i: (0, 0))
+    cum_spec = pl.BlockSpec((1, rows, WIDE), lambda i: (i, 0, 0))
+    state_spec = pl.BlockSpec((block, STATE), lambda i: (i, 0))
+    row_spec = pl.BlockSpec((1, block), lambda i: (0, i))
+    own_state = pl.pallas_call(
+        state_kernel,
+        grid=(steps,),
+        in_specs=[x_spec, proj_spec, cum_spec],
+        out_specs=state_spec,
+        out_shape=jax.ShapeDtypeStruct((width, STATE), BF16),
+        cost_estimate=pl.CostEstimate(
+            flops=2 * rows * width * STATE, bytes_accessed=4 * 2**20, transcendentals=rows * width
+        ),
+        name="own_state",
+    )(ssm_input, write_proj, cum_blocks)
+    quarter = head_local // GROUP
+    own_states = own_state.reshape(GROUP, quarter, HEAD_P, STATE)
+    own_decays = jnp.exp(cum[rows - 1]).reshape(GROUP, quarter)
+    states = jnp.stack(trade(lambda p: pick(own_states, p)))
+    decays = jnp.stack(trade(lambda p: pick(own_decays, p)))
+
+    part = pl.pallas_call(
+        local_kernel,
+        grid=(steps,),
+        in_specs=[
+            x_spec,
+            proj_spec,
+            proj_spec,
+            cum_spec,
+            pl.BlockSpec((WIDE, rows), lambda i: (i, 0)),
+            row_spec,
+        ],
+        out_specs=x_spec,
+        out_shape=jax.ShapeDtypeStruct((rows, width), F32),
+        compiler_params=pltpu.CompilerParams(vmem_limit_bytes=40 * 2**20),
+        cost_estimate=pl.CostEstimate(
+            flops=4 * rows * rows * width,
+            bytes_accessed=6 * 2**20,
+            transcendentals=rows * rows * head_local,
+        ),
+        name="mix_local",
+    )(ssm_input, write_proj, read_proj, cum_blocks, cum_t, jnp.repeat(skip_gain, HEAD_P)[None])
+
+    in_order = [
+        (pick(decays, place ^ k)[:, None, None], pick(states, place ^ k).astype(F32))
+        for k in range(GROUP)
+    ]
+    group_decay, group_state = in_order[0]
+    for decay, state in in_order[1:]:
+        group_decay, group_state = group_decay * decay, decay * group_state + state
+    before = jnp.zeros((quarter, HEAD_P, STATE), BF16)
+    for _ in range(groups - 1):
+        before = upward((group_decay * before.astype(F32) + group_state).astype(BF16))
+    prefix = [before.astype(F32)]
+    for decay, state in in_order[:-1]:
+        prefix.append(decay * prefix[-1] + state)
+    prefix = jnp.stack(prefix).astype(BF16)
+    back = jnp.stack(trade(lambda p: pick(prefix, p)))
+    start = jnp.concatenate([pick(back, place ^ g) for g in range(GROUP)])
+    gated, squares = pl.pallas_call(
+        gate_kernel,
+        grid=(steps,),
+        in_specs=[x_spec, x_spec, proj_spec, cum_spec, state_spec],
+        out_specs=[x_spec, proj_spec],
+        out_shape=[
+            jax.ShapeDtypeStruct((rows, width), F32),
+            jax.ShapeDtypeStruct((rows, 128), F32),
+        ],
+        compiler_params=pltpu.CompilerParams(vmem_limit_bytes=40 * 2**20),
+        cost_estimate=pl.CostEstimate(
+            flops=2 * rows * width * STATE, bytes_accessed=10 * 2**20, transcendentals=rows * width
+        ),
+        name="carry_and_gate",
+    )(part, gate_input, read_proj, cum_blocks, start.reshape(width, STATE))
+    own_square = jnp.sum(squares, axis=1)
+    square_total = own_square + lax.ppermute(own_square, "heads", [(0, 1), (1, 0)])
+    row_scale = lax.rsqrt(square_total / (SSM_HEADS * HEAD_P) + 1e-05)
+    ssm_out = (gated * row_scale[:, None] * norm_gain[None, :]).astype(BF16)
+
+    state = None
+    for step in range(groups):
+        info = jnp.stack([place, (level >= step).astype(jnp.int32)]).astype(jnp.int32)
+        following = upward(keys_values) if step < groups - 1 else None
+        state = attend_step(info, query, keys_values, state, step == groups - 1)
+        keys_values = following
+    outs = trade(lambda p: pick(state, place ^ p))
+    outs = jnp.stack(outs)
+    attn_out = jnp.concatenate([pick(outs, place ^ g) for g in range(GROUP)], axis=1)
+    return (ssm_out, attn_out)
+
+
 def solution(mesh):
     in_specs = (
         P("ctx", "heads"),
@@ -204,4 +521,7 @@
         P("ctx", "heads"),
     )
     out_specs = (P("ctx", "heads"), P("ctx", "heads"))
-    return jax.shard_map(body, mesh=mesh, in_specs=in_specs, out_specs=out_specs, check_vma=False)
+    ctx, heads = mesh.shape["ctx"], mesh.shape["heads"]
+    grouped = ctx % GROUP == 0 and ctx > GROUP and KV_HEADS // heads == GROUP and heads == 2
+    chosen = functools.partial(grouped_body, ctx) if grouped else body
+    return jax.shard_map(chosen, mesh=mesh, in_specs=in_specs, out_specs=out_specs, check_vma=False)

time: 572 us -> 137 us (0.24); the launches traced: 564 us -> 136 us
  waiting for transfers between devices: 286 us -> 29.1 us
  matrix products: 90 us -> 0.24 us
  Pallas kernels: 0 us -> 51.4 us
  other arithmetic: 60.3 us -> 10.6 us
  local copies, waits for them, and re-layouts: 53.2 us -> 12.2 us
  blocking collectives: 36.7 us -> 0 us
  starting transfers between devices: 0.11 us -> 31.2 us
  loops' own time: 22.5 us -> 0 us
  between operations: 15.1 us -> 1.24 us
    all_gather x3 -> x0, waiting for transfers between devices: 285 us -> none  [the longest x1 233 us: carried_in(): gathered = jax.tree.map(lambda a: lax.all_gather(a, axis), part)]
    dot_general x30 -> x1, matrix products: 90 us -> 0.24 us  [grouped_body(): cum = jnp.dot(causal, log_decay, precision=lax.Precision.HIGHEST)]
    pallas_call x0 -> x7, Pallas kernels: none -> 51.4 us  [the longest x4 35.2 us: attend_step(): pl.pallas_call(functools.partial(attend_kernel, rows, first, last), grid=...]
    add x54 -> x0, other arithmetic: 38.3 us -> none  [the longest x15 29.4 us: chain_combine(): later[0][:, None, None] * earlier[1] + later[1]]
    unnamed x1 -> x0, blocking collectives: 34.2 us -> none
    ppermute x0 -> x25, starting transfers between devices: none -> 31.2 us  [the longest x18 23.2 us: swap(): return lax.ppermute(piece, 'ctx', [(i, i ^ j) for i in range(ctx_size)])]
    ppermute x0 -> x25, waiting for transfers between devices: none -> 29.1 us  [the longest x6 15.7 us: upward(): return jax.tree.map(lambda a: lax.ppermute(a, 'ctx', pairs), piece)]
    reshape x8 -> x1, local copies, waits for them, and re-layouts: 26.3 us -> 1.16 us  [grouped_body(): cum_blocks = jnp.transpose(cum.reshape(rows, steps, WIDE), (1, 0, 2))]
  transfers between devices with their start and end apart: 3 -> 25, of which waited for: 2 -> 7; matrix products, arithmetic and copies ran while one was open for 26% -> 9% of each run, Pallas kernels for 0% -> 30%
where the time goes in v1:
time: 137 us; the launch traced here: 136 us
  Pallas kernels  51.4 us (38%)
  starting transfers between devices  31.2 us (23%)
  waiting for transfers between devices  29.1 us (21%)
  local copies, waits for them, and re-layouts  12.2 us (9%)
  other arithmetic  10.6 us (8%)
    pallas_call x4, Pallas kernels, attend_step(): pl.pallas_call(functools.partial(attend_kernel, rows, first, last), grid=...  35.2 us
    ppermute x18, starting transfers between devices, swap(): return lax.ppermute(piece, 'ctx', [(i, i ^ j) for i in range(ctx_size)])  23.2 us
    ppermute x6, waiting for transfers between devices, upward(): return jax.tree.map(lambda a: lax.ppermute(a, 'ctx', pairs), piece)  15.7 us
    ppermute x18, waiting for transfers between devices, swap(): return lax.ppermute(piece, 'ctx', [(i, i ^ j) for i in range(ctx_size)])  13.4 us
    ppermute x6, starting transfers between devices, upward(): return jax.tree.map(lambda a: lax.ppermute(a, 'ctx', pairs), piece)  7.91 us
    pallas_call x1, Pallas kernels, grouped_body(): pl.pallas_call(state_kernel, grid=(steps,), in_specs=[x_spec, proj_spec,...  7.46 us
    unnamed x36, local copies, waits for them, and re-layouts  6.73 us
    pallas_call x1, Pallas kernels, grouped_body(): pl.pallas_call(local_kernel, grid=(steps,), in_specs=[x_spec, proj_spec,...  5.06 us
  transfers between devices with their start and end apart: 25, of which 7 were waited for; matrix products, arithmetic and copies ran while one was open for 9% of the time, Pallas kernels for 30%

profile of v1, /device:TPU:24, one launch (start us, length us, event | category | flops | bytes accessed | tf_op | source)
XLA Modules:
  0.0 135.9 jit_solution(16941008236515948799)
XLA Ops:
  2.9 7.5 %own_state.1 = bf16[4096,128]{1,0:T(8,128)(2,1)} custom-call(bf16[192,4096]{1,0:T(8,128)(2,1)} %x_ref.3, bf16[192,128]{1,0:T(8,128)(2,1)} %write_ref.3, f32[8,192,8]{2,1,0:T(8,128)} %bitcast.114), custom_call_target="tpu_custom_call" | custom-call | flops 201326592 | bytes 4194304 | tf_op jit(solution)/shard_map/own_state/pallas_call | solution.py:423
  11.7 1.6 %collective-permute-start.3 = (bf16[16,64,128]{2,1,0:T(8,128)(2,1)S(1)}, bf16[16,64,128]{2,1,0:T(8,128)(2,1)S(1)}, u32[]{:S(2)}, u32[]{:S(2)}) collective-permute-start(bf16[16,64,128]{2,1,0:T(8,128)(2,1)S(1)} %get-tuple-element.46), channel_id=1, source_target_pairs={{0,2},{2,0},{4,6},{6,4},{8,10},{10,8},{12,14},{14,12},{16,18},{18,... | collective-permute-start | bytes 786440 | tf_op jit(solution)/shard_map/ppermute | solution.py:385
  13.3 1.5 %collective-permute-start.4 = (bf16[16,64,128]{2,1,0:T(8,128)(2,1)S(1)}, bf16[16,64,128]{2,1,0:T(8,128)(2,1)S(1)}, u32[]{:S(2)}, u32[]{:S(2)}) collective-permute-start(bf16[16,64,128]{2,1,0:T(8,128)(2,1)S(1)} %get-tuple-element.45), channel_id=1, source_target_pairs={{0,4},{2,6},{4,0},{6,2},{8,12},{10,14},{12,8},{14,10},{16,20},{18,... | collective-permute-start | bytes 786440 | tf_op jit(solution)/shard_map/ppermute | solution.py:385
  15.6 1.6 %collective-permute-start = (f32[16]{0:T(128)S(1)}, f32[16]{0:T(128)S(1)}, u32[]{:S(2)}, u32[]{:S(2)}) collective-permute-start(f32[16]{0:T(128)S(1)} %get-tuple-element.70), channel_id=1, source_target_pairs={{0,2},{2,0},{4,6},{6,4},{8,10},{10,8},{12,14},{14,12},{16,18},{18,... | collective-permute-start | bytes 200 | tf_op jit(solution)/shard_map/ppermute | solution.py:385
  19.7 5.8 %collective-permute-done = f32[16]{0:T(128)S(1)} collective-permute-done((f32[16]{0:T(128)S(1)}, f32[16]{0:T(128)S(1)}, u32[]{:S(2)}, u32[]{:S(2)}) %collective-permute-start) | collective-permute-done | bytes 96 | tf_op jit(solution)/shard_map/ppermute | solution.py:385
  25.5 2.4 %collective-permute-start.2 = (f32[16]{0:T(128)S(1)}, f32[16]{0:T(128)S(1)}, u32[]{:S(2)}, u32[]{:S(2)}) collective-permute-start(f32[16]{0:T(128)S(1)} %get-tuple-element.68), channel_id=1, source_target_pairs={{0,6},{2,4},{4,2},{6,0},{8,14},{10,12},{12,10},{14,8},{16,22},{18,... | collective-permute-start | bytes 200 | tf_op jit(solution)/shard_map/ppermute | solution.py:385
  29.9 1.5 %collective-permute-start.17 = (bf16[192,256]{1,0:T(8,128)(2,1)S(1)}, bf16[192,256]{1,0:T(8,128)(2,1)S(1)}, u32[]{:S(2)}, u32[]{:S(2)}) collective-permute-start(bf16[192,256]{1,0:T(8,128)(2,1)S(1)} %pad_maximum_fusion.9), channel_id=1, source_target_pairs={{0,4},{2,6},{4,0},{6,2},{8,12},{10,14},{12,8},{14,10},{16,20},{18,... | collective-permute-start | bytes 294920 | tf_op jit(solution)/shard_map/ppermute | solution.py:385
  35.5 1.5 %collective-permute-start.14 = (bf16[192,512]{1,0:T(8,128)(2,1)}, bf16[192,512]{1,0:T(8,128)(2,1)}, u32[]{:S(2)}, u32[]{:S(2)}) collective-permute-start(bf16[192,512]{1,0:T(8,128)(2,1)} %get-tuple-element.58), channel_id=1, source_target_pairs={{0,4},{2,6},{4,0},{6,2},{8,12},{10,14},{12,8},{14,10},{16,20},{18,... | collective-permute-start | bytes 589832 | tf_op jit(solution)/shard_map/ppermute | solution.py:385
  39.8 4.8 %collective-permute-done.6 = bf16[16,64,128]{2,1,0:T(8,128)(2,1)S(1)} collective-permute-done((bf16[16,64,128]{2,1,0:T(8,128)(2,1)S(1)}, bf16[16,64,128]{2,1,0:T(8,128)(2,1)S(1)}, u32[]{:S(2)}, u32[]{:S(2)}) %collective-permute-start.6) | collective-permute-done | bytes 262176 | tf_op jit(solution)/shard_map/ppermute | solution.py:389
  46.5 6.7 %collective-permute-done.19.refs_2_ = bf16[4,192,256]{2,1,0:T(8,128)(2,1)} collective-permute-done((bf16[4,192,256]{2,1,0:T(8,128)(2,1)S(1)}, bf16[4,192,256]{2,1,0:T(8,128)(2,1)}, u32[]{:S(2)}, u32[]{:S(2)}) %collective-permute-start.19) | collective-permute-done | bytes 393248 | tf_op jit(solution)/shard_map/ppermute | solution.py:389
  54.4 4.2 %collective-permute-done.7 = bf16[16,64,128]{2,1,0:T(8,128)(2,1)S(1)} collective-permute-done((bf16[16,64,128]{2,1,0:T(8,128)(2,1)S(1)}, bf16[16,64,128]{2,1,0:T(8,128)(2,1)S(1)}, u32[]{:S(2)}, u32[]{:S(2)}) %collective-permute-start.7) | collective-permute-done | bytes 262176 | tf_op jit(solution)/shard_map/ppermute | solution.py:389
  63.4 5.1 %mix_local.1.part_ref = f32[192,4096]{1,0:T(8,128)S(1)} custom-call(bf16[192,4096]{1,0:T(8,128)(2,1)S(1)} %copy-done.3, bf16[192,128]{1,0:T(8,128)(2,1)S(1)} %copy-done.10, bf16[192,128]{1,0:T(8,128)(2,1)S(1)} %copy-done.9, f32[8,192,8]{2,1,0:T(8,128)S(1)} %bitcast.115, f32[64,192]{1,0:T(8,128)S(1)} %bitcast.119, f32[1,4096]{1,0:T(1,128)S(1)} %broadcast_in_dim_reshape.3.skip_ref), custom_call_target="tpu_custom_call" | custom-call | flops 603979776 | bytes 6291456 | tf_op jit(solution)/shard_map/mix_local/pallas_call | solution.py:440
  69.9 7.1 %attend.4 = (f32[4,4,192,128]{3,2,1,0:T(8,128)S(1)}, f32[4,4,192,128]{3,2,1,0:T(8,128)S(1)}, f32[4,4,192,128]{3,2,1,0:T(8,128)S(1)}) custom-call(s32[2]{0:T(128)S(1)} %pad_add_fusion.3.refs_0_, bf16[4,192,512]{2,1,0:T(8,128)(2,1)S(1)} %pad_maximum_fusion.4.refs_1_, bf16[4,192,256]{2,1,0:T(8,128)(2,1)S(1)} %copy-done.8), custom_call_target="tpu_custom_call" | custom-call | flops 1207959552 | bytes 12582912 | tf_op jit(solution)/shard_map/attend/pallas_call | solution.py:341
  81.0 2.0 %collective-permute-start.9 = (bf16[16,64,128]{2,1,0:T(8,128)(2,1)S(1)}, bf16[16,64,128]{2,1,0:T(8,128)(2,1)S(1)}, u32[]{:S(2)}, u32[]{:S(2)}) collective-permute-start(bf16[16,64,128]{2,1,0:T(8,128)(2,1)S(1)} %get-tuple-element.42), channel_id=1, source_target_pairs={{0,2},{2,0},{4,6},{6,4},{8,10},{10,8},{12,14},{14,12},{16,18},{18,... | collective-permute-start | bytes 786440 | tf_op jit(solution)/shard_map/ppermute | solution.py:385
  83.0 1.6 %collective-permute-start.10 = (bf16[16,64,128]{2,1,0:T(8,128)(2,1)S(1)}, bf16[16,64,128]{2,1,0:T(8,128)(2,1)S(1)}, u32[]{:S(2)}, u32[]{:S(2)}) collective-permute-start(bf16[16,64,128]{2,1,0:T(8,128)(2,1)S(1)} %get-tuple-element.41), channel_id=1, source_target_pairs={{0,4},{2,6},{4,0},{6,2},{8,12},{10,14},{12,8},{14,10},{16,20},{18,... | collective-permute-start | bytes 786440 | tf_op jit(solution)/shard_map/ppermute | solution.py:385
  84.6 9.5 %attend.5 = (f32[4,4,192,128]{3,2,1,0:T(8,128)S(1)}, f32[4,4,192,128]{3,2,1,0:T(8,128)S(1)}, f32[4,4,192,128]{3,2,1,0:T(8,128)S(1)}) custom-call(s32[2]{0:T(128)S(1)} %pad_add_fusion.2.refs_0_, bf16[4,192,512]{2,1,0:T(8,128)(2,1)S(1)} %pad_maximum_fusion.4.refs_1_, bf16[4,192,256]{2,1,0:T(8,128)(2,1)} %collective-permute-done.19.refs_2_, ...), custom_call_target="tpu_custom_call" | custom-call | flops 1207959552 | bytes 12582912 | tf_op jit(solution)/shard_map/attend/pallas_call | solution.py:341
  94.1 9.5 %attend.6 = (f32[4,4,192,128]{3,2,1,0:T(8,128)S(1)}, f32[4,4,192,128]{3,2,1,0:T(8,128)S(1)}, f32[4,4,192,128]{3,2,1,0:T(8,128)S(1)}) custom-call(s32[2]{0:T(128)S(1)} %pad_add_fusion.1.refs_0_, bf16[4,192,512]{2,1,0:T(8,128)(2,1)S(1)} %pad_maximum_fusion.4.refs_1_, bf16[4,192,256]{2,1,0:T(8,128)(2,1)} %collective-permute-done.20.refs_2_, ...), custom_call_target="tpu_custom_call" | custom-call | flops 1207959552 | bytes 12582912 | tf_op jit(solution)/shard_map/attend/pallas_call | solution.py:341
  103.6 9.1 %attend.7 = bf16[4,192,512]{2,1,0:T(8,128)(2,1)S(1)} custom-call(s32[2]{0:T(128)S(1)} %pad_add_fusion.refs_0_, bf16[4,192,512]{2,1,0:T(8,128)(2,1)S(1)} %pad_maximum_fusion.4.refs_1_, bf16[4,192,256]{2,1,0:T(8,128)(2,1)S(1)} %collective-permute-done.21.refs_2_, f32[4,4,192,128]{3,2,1,0:T(8,128)S(1)} %get-tuple-element.21.refs_3_, ...), custom_call_target="tpu_custom_call" | custom-call | flops 1207959552 | bytes 12582912 | tf_op jit(solution)/shard_map/attend/pallas_call | solution.py:341
  114.8 3.7 %carry_and_gate.1 = (f32[192,4096]{1,0:T(8,128)S(1)}, f32[192,128]{1,0:T(8,128)S(1)}) custom-call(f32[192,4096]{1,0:T(8,128)S(1)} %mix_local.1.part_ref, bf16[192,4096]{1,0:T(8,128)(2,1)S(1)} %copy-done.6, bf16[192,128]{1,0:T(8,128)(2,1)S(1)} %copy-done.9, f32[8,192,8]{2,1,0:T(8,128)S(1)} %bitcast.116, bf16[4096,128]{1,0:T(8,128)(2,1)S(1)} %bitcast.117), custom_call_target="tpu_custom_call" | custom-call | flops 201326592 | bytes 10485760 | tf_op jit(solution)/shard_map/carry_and_gate/pallas_call | solution.py:478
  118.5 1.6 %copy-done.4 = f32[192,4096]{1,0:T(8,128)} copy-done((f32[192,4096]{1,0:T(8,128)}, f32[192,4096]{1,0:T(8,128)S(1)}, u32[]{:S(2)}) %copy-start.4) | copy-done | bytes 3145752
  121.6 2.0 %collective-permute-start.22 = (bf16[192,512]{1,0:T(8,128)(2,1)S(1)}, bf16[192,512]{1,0:T(8,128)(2,1)S(1)}, u32[]{:S(2)}, u32[]{:S(2)}) collective-permute-start(bf16[192,512]{1,0:T(8,128)(2,1)S(1)} %get-tuple-element.54), channel_id=1, source_target_pairs={{0,2},{2,0},{4,6},{6,4},{8,10},{10,8},{12,14},{14,12},{16,18},{18,... | collective-permute-start | bytes 589832 | tf_op jit(solution)/shard_map/ppermute | solution.py:385
  123.6 1.6 %collective-permute-start.23 = (bf16[192,512]{1,0:T(8,128)(2,1)S(1)}, bf16[192,512]{1,0:T(8,128)(2,1)S(1)}, u32[]{:S(2)}, u32[]{:S(2)}) collective-permute-start(bf16[192,512]{1,0:T(8,128)(2,1)S(1)} %get-tuple-element.53), channel_id=1, source_target_pairs={{0,4},{2,6},{4,0},{6,2},{8,12},{10,14},{12,8},{14,10},{16,20},{18,... | collective-permute-start | bytes 589832 | tf_op jit(solution)/shard_map/ppermute | solution.py:385
  125.2 3.5 %multiply_convert_fusion = bf16[192,4096]{1,0:T(8,128)(2,1)} fusion(f32[192,4096]{1,0:T(8,128)} %copy-done.4, f32[4096]{0:T(1024)S(1)} %copy-done.16, f32[192]{0:T(256)S(1)} %add_rsqrt_fusion), kind=kLoop, calls=%fused_computation | loop fusion | flops 2359296 | bytes 4735744 | tf_op jit(solution)/shard_map/convert_element_type | solution.py:496
  129.4 5.3 %collective-permute-done.23 = bf16[192,512]{1,0:T(8,128)(2,1)S(1)} collective-permute-done((bf16[192,512]{1,0:T(8,128)(2,1)S(1)}, bf16[192,512]{1,0:T(8,128)(2,1)S(1)}, u32[]{:S(2)}, u32[]{:S(2)}) %collective-permute-start.23) | collective-permute-done | bytes 196640 | tf_op jit(solution)/shard_map/ppermute | solution.py:385
  (108 shorter events, 34.3 us)
Async XLA Ops:
  11.7 19.8 %collective-permute-start.3 = (bf16[16,64,128]{2,1,0:T(8,128)(2,1)S(1)}, bf16[16,64,128]{2,1,0:T(8,128)(2,1)S(1)}, u32[]{:S(2)}, u32[]{:S(2)}) collective-permute-start(bf16[16,64,128]{2,1,0:T(8,128)(2,1)S(1)} %get-tuple-element.46), channel_id=1, source_target_pairs={{0,2},{2,0},{4,6},{6,4},{8,10},{10,8},{12,14},{14,12},{16,18},{18,... | collective-permute-start | bytes 786440 | tf_op jit(solution)/shard_map/ppermute | solution.py:385
  13.3 19.7 %collective-permute-start.4 = (bf16[16,64,128]{2,1,0:T(8,128)(2,1)S(1)}, bf16[16,64,128]{2,1,0:T(8,128)(2,1)S(1)}, u32[]{:S(2)}, u32[]{:S(2)}) collective-permute-start(bf16[16,64,128]{2,1,0:T(8,128)(2,1)S(1)} %get-tuple-element.45), channel_id=1, source_target_pairs={{0,4},{2,6},{4,0},{6,2},{8,12},{10,14},{12,8},{14,10},{16,20},{18,... | collective-permute-start | bytes 786440 | tf_op jit(solution)/shard_map/ppermute | solution.py:385
  14.8 18.7 %collective-permute-start.5 = (bf16[16,64,128]{2,1,0:T(8,128)(2,1)S(1)}, bf16[16,64,128]{2,1,0:T(8,128)(2,1)S(1)}, u32[]{:S(2)}, u32[]{:S(2)}) collective-permute-start(bf16[16,64,128]{2,1,0:T(8,128)(2,1)S(1)} %get-tuple-element.44), channel_id=1, source_target_pairs={{0,6},{2,4},{4,2},{6,0},{8,14},{10,12},{12,10},{14,8},{16,22},{18,... | collective-permute-start | bytes 786440 | tf_op jit(solution)/shard_map/ppermute | solution.py:385
  15.6 9.9 %collective-permute-start = (f32[16]{0:T(128)S(1)}, f32[16]{0:T(128)S(1)}, u32[]{:S(2)}, u32[]{:S(2)}) collective-permute-start(f32[16]{0:T(128)S(1)} %get-tuple-element.70), channel_id=1, source_target_pairs={{0,2},{2,0},{4,6},{6,4},{8,10},{10,8},{12,14},{14,12},{16,18},{18,... | collective-permute-start | bytes 200 | tf_op jit(solution)/shard_map/ppermute | solution.py:385
  17.1 10.8 %collective-permute-start.1 = (f32[16]{0:T(128)S(1)}, f32[16]{0:T(128)S(1)}, u32[]{:S(2)}, u32[]{:S(2)}) collective-permute-start(f32[16]{0:T(128)S(1)} %get-tuple-element.69), channel_id=1, source_target_pairs={{0,4},{2,6},{4,0},{6,2},{8,12},{10,14},{12,8},{14,10},{16,20},{18,... | collective-permute-start | bytes 200 | tf_op jit(solution)/shard_map/ppermute | solution.py:385
  27.9 7.6 %collective-permute-start.16 = (bf16[192,256]{1,0:T(8,128)(2,1)S(1)}, bf16[192,256]{1,0:T(8,128)(2,1)S(1)}, u32[]{:S(2)}, u32[]{:S(2)}) collective-permute-start(bf16[192,256]{1,0:T(8,128)(2,1)S(1)} %pad_maximum_fusion.8), channel_id=1, source_target_pairs={{0,2},{2,0},{4,6},{6,4},{8,10},{10,8},{12,14},{14,12},{16,18},{18,... | collective-permute-start | bytes 294920 | tf_op jit(solution)/shard_map/ppermute | solution.py:385
  29.9 7.1 %collective-permute-start.17 = (bf16[192,256]{1,0:T(8,128)(2,1)S(1)}, bf16[192,256]{1,0:T(8,128)(2,1)S(1)}, u32[]{:S(2)}, u32[]{:S(2)}) collective-permute-start(bf16[192,256]{1,0:T(8,128)(2,1)S(1)} %pad_maximum_fusion.9), channel_id=1, source_target_pairs={{0,4},{2,6},{4,0},{6,2},{8,12},{10,14},{12,8},{14,10},{16,20},{18,... | collective-permute-start | bytes 294920 | tf_op jit(solution)/shard_map/ppermute | solution.py:385
  31.5 7.0 %collective-permute-start.18 = (bf16[192,256]{1,0:T(8,128)(2,1)S(1)}, bf16[192,256]{1,0:T(8,128)(2,1)S(1)}, u32[]{:S(2)}, u32[]{:S(2)}) collective-permute-start(bf16[192,256]{1,0:T(8,128)(2,1)S(1)} %pad_maximum_fusion.10), channel_id=1, source_target_pairs={{0,6},{2,4},{4,2},{6,0},{8,14},{10,12},{12,10},{14,8},{16,22},{18,... | collective-permute-start | bytes 294920 | tf_op jit(solution)/shard_map/ppermute | solution.py:385
  33.0 35.5 %collective-permute-start.13 = (bf16[192,512]{1,0:T(8,128)(2,1)}, bf16[192,512]{1,0:T(8,128)(2,1)}, u32[]{:S(2)}, u32[]{:S(2)}) collective-permute-start(bf16[192,512]{1,0:T(8,128)(2,1)} %get-tuple-element.56), channel_id=1, source_target_pairs={{0,2},{2,0},{4,6},{6,4},{8,10},{10,8},{12,14},{14,12},{16,18},{18,... | collective-permute-start | bytes 589832 | tf_op jit(solution)/shard_map/ppermute | solution.py:385
  34.0 10.6 %collective-permute-start.6 = (bf16[16,64,128]{2,1,0:T(8,128)(2,1)S(1)}, bf16[16,64,128]{2,1,0:T(8,128)(2,1)S(1)}, u32[]{:S(2)}, u32[]{:S(2)}) collective-permute-start(bf16[16,64,128]{2,1,0:T(8,128)(2,1)S(1)} %get-tuple-element.24), channel_id=1, source_target_pairs={{0,8},{2,10},{4,12},{6,14},{8,16},{10,18},{12,20},{14,22},{16,24},... | collective-permute-start | bytes 786440 | tf_op jit(solution)/shard_map/ppermute | solution.py:389
  35.5 33.0 %collective-permute-start.14 = (bf16[192,512]{1,0:T(8,128)(2,1)}, bf16[192,512]{1,0:T(8,128)(2,1)}, u32[]{:S(2)}, u32[]{:S(2)}) collective-permute-start(bf16[192,512]{1,0:T(8,128)(2,1)} %get-tuple-element.58), channel_id=1, source_target_pairs={{0,4},{2,6},{4,0},{6,2},{8,12},{10,14},{12,8},{14,10},{16,20},{18,... | collective-permute-start | bytes 589832 | tf_op jit(solution)/shard_map/ppermute | solution.py:385
  37.0 31.5 %collective-permute-start.15 = (bf16[192,512]{1,0:T(8,128)(2,1)}, bf16[192,512]{1,0:T(8,128)(2,1)}, u32[]{:S(2)}, u32[]{:S(2)}) collective-permute-start(bf16[192,512]{1,0:T(8,128)(2,1)} %get-tuple-element.57), channel_id=1, source_target_pairs={{0,6},{2,4},{4,2},{6,0},{8,14},{10,12},{12,10},{14,8},{16,22},{18,... | collective-permute-start | bytes 589832 | tf_op jit(solution)/shard_map/ppermute | solution.py:385
  38.5 14.6 %collective-permute-start.19 = (bf16[4,192,256]{2,1,0:T(8,128)(2,1)S(1)}, bf16[4,192,256]{2,1,0:T(8,128)(2,1)}, u32[]{:S(2)}, u32[]{:S(2)}) collective-permute-start(bf16[4,192,256]{2,1,0:T(8,128)(2,1)S(1)} %pad_maximum_fusion.7.refs_2_), channel_id=1, source_target_pairs={{0,8},{2,10},{4,12},{6,14},{8,16},{10,18},{12,20},{14,22},{16,24},... | collective-permute-start | bytes 1179656 | tf_op jit(solution)/shard_map/ppermute | solution.py:389
  44.8 13.9 %collective-permute-start.7 = (bf16[16,64,128]{2,1,0:T(8,128)(2,1)S(1)}, bf16[16,64,128]{2,1,0:T(8,128)(2,1)S(1)}, u32[]{:S(2)}, u32[]{:S(2)}) collective-permute-start(bf16[16,64,128]{2,1,0:T(8,128)(2,1)S(1)} %add_convert_fusion.1), channel_id=1, source_target_pairs={{0,8},{2,10},{4,12},{6,14},{8,16},{10,18},{12,20},{14,22},{16,24},... | collective-permute-start | bytes 786440 | tf_op jit(solution)/shard_map/ppermute | solution.py:389
  53.2 23.9 %collective-permute-start.20 = (bf16[4,192,256]{2,1,0:T(8,128)(2,1)}, bf16[4,192,256]{2,1,0:T(8,128)(2,1)}, u32[]{:S(2)}, u32[]{:S(2)}) collective-permute-start(bf16[4,192,256]{2,1,0:T(8,128)(2,1)} %collective-permute-done.19.refs_2_), channel_id=1, source_target_pairs={{0,8},{2,10},{4,12},{6,14},{8,16},{10,18},{12,20},{14,22},{16,24},... | collective-permute-start | bytes 1179656 | tf_op jit(solution)/shard_map/ppermute | solution.py:389
  59.5 19.0 %collective-permute-start.8 = (bf16[16,64,128]{2,1,0:T(8,128)(2,1)}, bf16[16,64,128]{2,1,0:T(8,128)(2,1)}, u32[]{:S(2)}, u32[]{:S(2)}) collective-permute-start(bf16[16,64,128]{2,1,0:T(8,128)(2,1)} %add_convert_fusion), channel_id=1, source_target_pairs={{0,8},{2,10},{4,12},{6,14},{8,16},{10,18},{12,20},{14,22},{16,24},... | collective-permute-start | bytes 786440 | tf_op jit(solution)/shard_map/ppermute | solution.py:389
  77.0 26.6 %collective-permute-start.21 = (bf16[4,192,256]{2,1,0:T(8,128)(2,1)}, bf16[4,192,256]{2,1,0:T(8,128)(2,1)S(1)}, u32[]{:S(2)}, u32[]{:S(2)}) collective-permute-start(bf16[4,192,256]{2,1,0:T(8,128)(2,1)} %collective-permute-done.20.refs_2_), channel_id=1, source_target_pairs={{0,8},{2,10},{4,12},{6,14},{8,16},{10,18},{12,20},{14,22},{16,24},... | collective-permute-start | bytes 1179656 | tf_op jit(solution)/shard_map/ppermute | solution.py:389
  81.0 31.7 %collective-permute-start.9 = (bf16[16,64,128]{2,1,0:T(8,128)(2,1)S(1)}, bf16[16,64,128]{2,1,0:T(8,128)(2,1)S(1)}, u32[]{:S(2)}, u32[]{:S(2)}) collective-permute-start(bf16[16,64,128]{2,1,0:T(8,128)(2,1)S(1)} %get-tuple-element.42), channel_id=1, source_target_pairs={{0,2},{2,0},{4,6},{6,4},{8,10},{10,8},{12,14},{14,12},{16,18},{18,... | collective-permute-start | bytes 786440 | tf_op jit(solution)/shard_map/ppermute | solution.py:385
  83.0 29.7 %collective-permute-start.10 = (bf16[16,64,128]{2,1,0:T(8,128)(2,1)S(1)}, bf16[16,64,128]{2,1,0:T(8,128)(2,1)S(1)}, u32[]{:S(2)}, u32[]{:S(2)}) collective-permute-start(bf16[16,64,128]{2,1,0:T(8,128)(2,1)S(1)} %get-tuple-element.41), channel_id=1, source_target_pairs={{0,4},{2,6},{4,0},{6,2},{8,12},{10,14},{12,8},{14,10},{16,20},{18,... | collective-permute-start | bytes 786440 | tf_op jit(solution)/shard_map/ppermute | solution.py:385
  84.5 28.2 %collective-permute-start.11 = (bf16[16,64,128]{2,1,0:T(8,128)(2,1)S(1)}, bf16[16,64,128]{2,1,0:T(8,128)(2,1)S(1)}, u32[]{:S(2)}, u32[]{:S(2)}) collective-permute-start(bf16[16,64,128]{2,1,0:T(8,128)(2,1)S(1)} %get-tuple-element.40), channel_id=1, source_target_pairs={{0,6},{2,4},{4,2},{6,0},{8,14},{10,12},{12,10},{14,8},{16,22},{18,... | collective-permute-start | bytes 786440 | tf_op jit(solution)/shard_map/ppermute | solution.py:385
  120.2 4.9 %collective-permute-start.12 = (f32[192]{0:T(256)S(1)}, f32[192]{0:T(256)S(1)}, u32[]{:S(2)}, u32[]{:S(2)}) collective-permute-start(f32[192]{0:T(256)S(1)} %reduce_sum.9), channel_id=1, source_target_pairs={{0,1},{1,0},{2,3},{3,2},{4,5},{5,4},{6,7},{7,6},{8,9},{9,8},{10,11... | collective-permute-start | bytes 2312 | tf_op jit(solution)/shard_map/ppermute | solution.py:494
  121.6 7.8 %collective-permute-start.22 = (bf16[192,512]{1,0:T(8,128)(2,1)S(1)}, bf16[192,512]{1,0:T(8,128)(2,1)S(1)}, u32[]{:S(2)}, u32[]{:S(2)}) collective-permute-start(bf16[192,512]{1,0:T(8,128)(2,1)S(1)} %get-tuple-element.54), channel_id=1, source_target_pairs={{0,2},{2,0},{4,6},{6,4},{8,10},{10,8},{12,14},{14,12},{16,18},{18,... | collective-permute-start | bytes 589832 | tf_op jit(solution)/shard_map/ppermute | solution.py:385
  123.6 11.2 %collective-permute-start.23 = (bf16[192,512]{1,0:T(8,128)(2,1)S(1)}, bf16[192,512]{1,0:T(8,128)(2,1)S(1)}, u32[]{:S(2)}, u32[]{:S(2)}) collective-permute-start(bf16[192,512]{1,0:T(8,128)(2,1)S(1)} %get-tuple-element.53), channel_id=1, source_target_pairs={{0,4},{2,6},{4,0},{6,2},{8,12},{10,14},{12,8},{14,10},{16,20},{18,... | collective-permute-start | bytes 589832 | tf_op jit(solution)/shard_map/ppermute | solution.py:385
  125.1 9.7 %collective-permute-start.24 = (bf16[192,512]{1,0:T(8,128)(2,1)S(1)}, bf16[192,512]{1,0:T(8,128)(2,1)S(1)}, u32[]{:S(2)}, u32[]{:S(2)}) collective-permute-start(bf16[192,512]{1,0:T(8,128)(2,1)S(1)} %get-tuple-element.52), channel_id=1, source_target_pairs={{0,6},{2,4},{4,2},{6,0},{8,14},{10,12},{12,10},{14,8},{16,22},{18,... | collective-permute-start | bytes 589832 | tf_op jit(solution)/shard_map/ppermute | solution.py:385
  (19 other events, 140.6 us)

commit v2 on v0

--- a/solution.py
+++ b/solution.py
@@ -1,6 +1,11 @@
+import functools
+import math
+
 import jax
 import jax.numpy as jnp
 from jax import lax
+from jax.experimental import pallas as pl
+from jax.experimental.pallas import tpu as pltpu
 from jax.sharding import PartitionSpec as P
 
 SSM_HEADS = 128
@@ -190,6 +195,524 @@
     return (ssm_out, attn_out)
 
 
+GROUP = 4
+WIDE = 8
+BLOCK = WIDE * HEAD_P
+CHAIN = 4
+F32 = jnp.float32
+BF16 = jnp.bfloat16
+LOG2E = math.log2(math.e)
+MESH = pl.DeviceIdType.MESH
+
+
+def xor_place(a, b):
+    a1, a0, b1, b0 = a // 2, a % 2, b // 2, b % 2
+    return 2 * (a1 + b1 - 2 * a1 * b1) + (a0 + b0 - 2 * a0 * b0)
+
+
+def lanes(start, size):
+    return pl.ds(pl.multiple_of(start, 128), size)
+
+
+def expand_heads(per_head):
+    first = lax.broadcasted_iota(jnp.int32, (WIDE, BLOCK), 0) * HEAD_P
+    column = lax.broadcasted_iota(jnp.int32, (WIDE, BLOCK), 1)
+    spread = jnp.where((column >= first) & (column < first + HEAD_P), 1.0, 0.0).astype(BF16)
+    high = per_head.astype(BF16)
+    low = (per_head - high.astype(F32)).astype(BF16)
+    return jnp.dot(high, spread, preferred_element_type=F32) + jnp.dot(
+        low, spread, preferred_element_type=F32
+    )
+
+
+def grouped_kernel(
+    groups,
+    x_ref,
+    gate_ref,
+    write_ref,
+    read_ref,
+    cum_ref,
+    cum_t_ref,
+    skip_ref,
+    gain_ref,
+    query_ref,
+    key_ref,
+    value_ref,
+    ssm_ref,
+    attn_ref,
+    kv_buf,
+    q_buf,
+    o_buf,
+    own_states,
+    states,
+    own_decays,
+    decays,
+    carry_in,
+    carry_out,
+    prefix,
+    start,
+    part,
+    top_buf,
+    sum_buf,
+    acc_buf,
+    square_own,
+    square_other,
+    kv_send,
+    kv_recv,
+    q_send,
+    q_recv,
+    state_send,
+    state_recv,
+    decay_send,
+    decay_recv,
+    up_send,
+    up_recv,
+    chain_send,
+    chain_recv,
+    prefix_send,
+    prefix_recv,
+    o_send,
+    o_recv,
+    square_send,
+    square_recv,
+):
+    rows = x_ref.shape[0]
+    width = x_ref.shape[1]
+    quarter = width // GROUP
+    blocks = width // BLOCK
+    own = lax.axis_index("ctx")
+    place, level = own % GROUP, own // GROUP
+    top = groups - 1
+    base = level * GROUP
+    peer_place = [xor_place(place, j) for j in range(GROUP)]
+    other = 1 - lax.axis_index("heads")
+
+    def remote(src, dst, send, recv, **device):
+        return pltpu.make_async_remote_copy(
+            src_ref=src,
+            dst_ref=dst,
+            send_sem=send,
+            recv_sem=recv,
+            device_id=device,
+            device_id_type=MESH,
+        )
+
+    def to_peer(j, src, dst, send, recv):
+        return remote(src, dst, send, recv, ctx=base + peer_place[j])
+
+    key_sets = key_ref.shape[1] // GROUP
+    query_sets = query_ref.shape[1] // GROUP
+
+    def kv_copies(j):
+        columns = lanes(peer_place[j] * key_sets, key_sets)
+        return [
+            to_peer(
+                j,
+                ref.at[:, columns],
+                kv_buf.at[0, j, :, pl.ds(k * key_sets, key_sets)],
+                kv_send.at[k, j - 1],
+                kv_recv.at[k, j - 1],
+            )
+            for k, ref in enumerate((key_ref, value_ref))
+        ]
+
+    def q_copy(j):
+        columns = lanes(peer_place[j] * query_sets, query_sets)
+        return to_peer(
+            j, query_ref.at[:, columns], q_buf.at[j], q_send.at[j - 1], q_recv.at[j - 1]
+        )
+
+    def state_copies(j):
+        return [
+            to_peer(
+                j, own_states.at[j], states.at[j], state_send.at[j - 1], state_recv.at[j - 1]
+            ),
+            to_peer(
+                j, own_decays.at[j], decays.at[j], decay_send.at[j - 1], decay_recv.at[j - 1]
+            ),
+        ]
+
+    def up_copy(step, j):
+        return remote(
+            kv_buf.at[step, j],
+            kv_buf.at[step + 1, j],
+            up_send.at[step, j],
+            up_recv.at[step, j],
+            ctx=lax.rem(own + GROUP, groups * GROUP),
+        )
+
+    piece = quarter // CHAIN
+
+    def chain_copy(c):
+        return remote(
+            carry_out.at[c],
+            carry_in.at[c],
+            chain_send.at[c],
+            chain_recv.at[c],
+            ctx=lax.rem(own + GROUP, groups * GROUP),
+        )
+
+    def prefix_copy(c, j, landing):
+        return to_peer(
+            j,
+            prefix.at[peer_place[j], c],
+            start.at[:, lanes(landing * quarter + c * piece, piece)],
+            prefix_send.at[c, j - 1],
+            prefix_recv.at[c, j - 1],
+        )
+
+    def o_copy(j, landing):
+        return to_peer(
+            j,
+            o_buf.at[j],
+            attn_ref.at[:, lanes(landing * query_sets, query_sets)],
+            o_send.at[j - 1],
+            o_recv.at[j - 1],
+        )
+
+    def square_copy():
+        return remote(square_own, square_other, square_send.at[0], square_recv.at[0], heads=other)
+
+    barrier = pltpu.get_barrier_semaphore()
+    for j in range(1, GROUP):
+        pl.semaphore_signal(
+            barrier, inc=1, device_id={"ctx": base + peer_place[j]}, device_id_type=MESH
+        )
+    pl.semaphore_signal(barrier, inc=1, device_id={"heads": other}, device_id_type=MESH)
+
+    for step in (GROUP, (groups - 1) * GROUP):
+        neighbour = lax.rem(own + step, groups * GROUP)
+        pl.semaphore_signal(barrier, inc=1, device_id={"ctx": neighbour}, device_id_type=MESH)
+    pl.semaphore_wait(barrier, GROUP + 2)
+
+    for j in range(1, GROUP):
+        for copy in kv_copies(j):
+            copy.start()
+    own_columns = lanes(place * key_sets, key_sets)
+    kv_buf[0, 0, :, 0:key_sets] = key_ref[:, own_columns]
+    kv_buf[0, 0, :, key_sets:] = value_ref[:, own_columns]
+
+    def state_block(j, b):
+        index = peer_place[j] * (quarter // BLOCK) + b
+        cum = cum_ref[index]
+        last = cum[rows - 1 :, :]
+        weight = expand_heads(jnp.exp(last - cum))
+        scaled = (x_ref[:, lanes(index * BLOCK, BLOCK)].astype(F32) * weight).astype(BF16)
+        state = lax.dot_general(
+            write_ref[...], scaled, (((0,), (0,)), ((), ())), preferred_element_type=F32
+        )
+        decay = expand_heads(jnp.exp(jnp.broadcast_to(last, (8, WIDE))))
+        columns = slice(b * BLOCK, (b + 1) * BLOCK)
+        if j == 0:
+            states[0, :, columns] = state.astype(BF16)
+            decays[0, :, columns] = decay
+        else:
+            own_states[j, :, columns] = state.astype(BF16)
+            own_decays[j, :, columns] = decay
+
+    for j in (3, 1, 2, 0):
+        for b in range(quarter // BLOCK):
+            state_block(j, b)
+        if j > 0:
+            for copy in state_copies(j):
+                copy.start()
+    for j in range(1, GROUP):
+        q_copy(j).start()
+    q_buf[0] = query_ref[:, lanes(place * query_sets, query_sets)]
+
+    def forward(step):
+        if step < groups - 1:
+
+            @pl.when((level >= step) & (level < top))
+            def _():
+                for j in range(GROUP):
+                    if step > 0:
+                        up_copy(step - 1, j).wait_recv()
+                    up_copy(step, j).start()
+
+        if step > 0:
+
+            @pl.when((level >= step) & (level == top))
+            def _():
+                for j in range(GROUP):
+                    up_copy(step - 1, j).wait_recv()
+
+    inner = lax.dot_general(
+        read_ref[...], write_ref[...], (((1,), (1,)), ((), ())), preferred_element_type=F32
+    )
+    later = lax.broadcasted_iota(jnp.int32, (rows, rows), 0)
+    earlier = lax.broadcasted_iota(jnp.int32, (rows, rows), 1)
+    inner = jnp.where(earlier <= later, inner, 0.0)
+    left = lax.broadcasted_iota(jnp.int32, (rows, 2 * HEAD_P), 1) < HEAD_P
+
+    def local_block(index, carry):
+        cum = cum_ref[index]
+        cum_t = cum_t_ref[index]
+        for pair in range(WIDE // 2):
+            columns = lanes(index * BLOCK + pair * 2 * HEAD_P, 2 * HEAD_P)
+            x_pair = x_ref[:, columns]
+            halves = []
+            for h in (2 * pair, 2 * pair + 1):
+                gap = cum[:, h : h + 1] - cum_t[h : h + 1, :]
+                mix = (jnp.exp(jnp.minimum(gap, 0.0)) * inner).astype(BF16)
+                halves.append(jnp.dot(mix, x_pair, preferred_element_type=F32))
+            mixed = jnp.where(left, halves[0], halves[1])
+            part[:, columns] = mixed + skip_ref[:, columns] * x_pair.astype(F32)
+        return carry
+
+    lax.fori_loop(0, blocks // 2, local_block, 0)
+    for j in range(1, GROUP):
+        for copy in kv_copies(j):
+            copy.wait_recv()
+    forward(0)
+    lax.fori_loop(blocks // 2, blocks, local_block, 0)
+
+    def chain():
+        for c in range(CHAIN):
+            columns = slice(c * piece, (c + 1) * piece)
+
+            @pl.when(level > 0)
+            def _():
+                chain_copy(c).wait_recv()
+
+            @pl.when(level == 0)
+            def _():
+                carry_in[c] = jnp.zeros(carry_in.shape[1:], BF16)
+
+            state = carry_in[c].astype(F32)
+            for k in range(GROUP):
+                prefix[k, c] = state.astype(BF16)
+                j = xor_place(place, k)
+                state = decays[j, 0:1, columns] * state + states[j, :, columns].astype(F32)
+            carry_out[c] = state.astype(BF16)
+
+            @pl.when(level < top)
+            def _():
+                chain_copy(c).start()
+
+            for j in range(1, GROUP):
+                prefix_copy(c, j, place).start()
+            start[:, lanes(place * quarter + c * piece, piece)] = prefix[place, c]
+
+    factor = LOG2E / math.sqrt(HEAD_DIM)
+    heads = query_sets // HEAD_DIM
+    key_count = GROUP * rows
+
+    def attend(step):
+        first = step == 0
+        keys = kv_buf[step, :, :, 0:HEAD_DIM].reshape(key_count, HEAD_DIM)
+        values = kv_buf[step, :, :, HEAD_DIM:].reshape(key_count, HEAD_DIM)
+        if first:
+            column = lax.broadcasted_iota(jnp.int32, (1, key_count), 1)
+            shift = place * rows
+            for j in range(1, GROUP):
+                shift = jnp.where(column >= j * rows, (peer_place[j] - j) * rows, shift)
+            positions = column + shift
+
+        def one(block, carry):
+            if first:
+                row = lax.broadcasted_iota(jnp.int32, (rows, 1), 0)
+                visible = positions <= row + xor_place(place, block) * rows
+            for h in range(heads):
+                at = block * heads + h
+                query = q_buf[block, :, h * HEAD_DIM : (h + 1) * HEAD_DIM]
+                scores = lax.dot_general(
+                    query, keys, (((1,), (1,)), ((), ())), preferred_element_type=F32
+                )
+                if first:
+                    scores = jnp.where(visible, scores, -1e30)
+                new_max = jnp.max(scores, axis=1, keepdims=True)
+                if not first:
+                    new_max = jnp.maximum(new_max, top_buf[at][:, :1])
+                weights = jnp.exp2((scores - new_max) * factor)
+                new_sum = weights[:, :HEAD_DIM]
+                for k in range(1, key_count // HEAD_DIM):
+                    new_sum = new_sum + weights[:, k * HEAD_DIM : (k + 1) * HEAD_DIM]
+                new_acc = jnp.dot(weights.astype(BF16), values, preferred_element_type=F32)
+                if not first:
+                    rescale = jnp.exp2((top_buf[at] - new_max) * factor)
+                    new_sum = new_sum + rescale * sum_buf[at]
+                    new_acc = new_acc + rescale * acc_buf[at]
+                top_buf[at] = jnp.broadcast_to(new_max, (rows, HEAD_DIM))
+                sum_buf[at] = new_sum
+                acc_buf[at] = new_acc
+            return carry
+
+        lax.fori_loop(0, GROUP, one, 0)
+
+    for j in range(1, GROUP):
+        for copy in state_copies(j):
+            copy.wait_recv()
+    pl.when(level == 0)(chain)
+    for j in range(1, GROUP):
+        q_copy(j).wait_recv()
+    attend(0)
+    for step in range(1, groups):
+        forward(step)
+        if step < groups - 1:
+            pl.when(level == step)(chain)
+        else:
+            pl.when(level == top)(chain)
+        pl.when(level >= step)(functools.partial(attend, step))
+
+    for j in (3, 1, 2, 0):
+        for h in range(heads):
+            total = jnp.sum(sum_buf[j * heads + h], axis=1, keepdims=True)
+            o_buf[j, :, h * HEAD_DIM : (h + 1) * HEAD_DIM] = (
+                acc_buf[j * heads + h] / total
+            ).astype(BF16)
+        if j > 0:
+            o_copy(j, place).start()
+    attn_ref[:, lanes(place * query_sets, query_sets)] = o_buf[0]
+
+    for c in range(CHAIN):
+        for j in range(1, GROUP):
+            prefix_copy(c, j, peer_place[j]).wait_recv()
+    square_own[...] = jnp.zeros(square_own.shape, F32)
+
+    def gate_block(index, carry):
+        columns = lanes(index * BLOCK, BLOCK)
+        carried = jnp.dot(read_ref[...], start[:, columns], preferred_element_type=F32)
+        gate = gate_ref[:, columns].astype(F32)
+        mixed = part[:, columns] + expand_heads(jnp.exp(cum_ref[index])) * carried
+        gated = mixed * (gate / (1.0 + jnp.exp(-gate)))
+        part[:, columns] = gated
+        square = gated * gated
+        total = square_own[...]
+        for k in range(BLOCK // 128):
+            total = total + square[:, k * 128 : (k + 1) * 128]
+        square_own[...] = total
+        return carry
+
+    lax.fori_loop(0, blocks, gate_block, 0)
+    square_copy().start()
+    square_copy().wait_recv()
+    squares = jnp.sum(square_own[...] + square_other[...], axis=1, keepdims=True)
+    row_scale = lax.rsqrt(squares / (SSM_HEADS * HEAD_P) + 1e-05)
+
+    def norm_block(index, carry):
+        columns = lanes(index * BLOCK, BLOCK)
+        ssm_ref[:, columns] = (part[:, columns] * row_scale * gain_ref[:, columns]).astype(BF16)
+        return carry
+
+    lax.fori_loop(0, blocks, norm_block, 0)
+
+    square_copy().wait_send()
+    for j in range(1, GROUP):
+        o_copy(j, peer_place[j]).wait_recv()
+        o_copy(j, place).wait_send()
+        q_copy(j).wait_send()
+        for copy in kv_copies(j) + state_copies(j):
+            copy.wait_send()
+        for c in range(CHAIN):
+            prefix_copy(c, j, place).wait_send()
+    for step in range(groups - 1):
+
+        @pl.when((level >= step) & (level < top))
+        def _():
+            for j in range(GROUP):
+                up_copy(step, j).wait_send()
+
+    @pl.when(level < top)
+    def _():
+        for c in range(CHAIN):
+            chain_copy(c).wait_send()
+
+
+def grouped_body(
+    groups,
+    ssm_input,
+    gate_input,
+    write_proj,
+    read_proj,
+    log_decay,
+    skip_gain,
+    norm_gain,
+    query_rows,
+    key_rows,
+    value_rows,
+):
+    rows, width = ssm_input.shape
+    steps = width // BLOCK
+    quarter = width // GROUP
+    causal = (jnp.arange(rows)[:, None] >= jnp.arange(rows)[None, :]).astype(F32)
+    cum = jnp.dot(causal, log_decay, precision=lax.Precision.HIGHEST)
+    cum_blocks = jnp.transpose(cum.reshape(rows, steps, WIDE), (1, 0, 2))
+    cum_t = cum.T.reshape(steps, WIDE, rows)
+    query_sets = query_rows.shape[1] // GROUP
+    pairs = 2 * key_rows.shape[1] // GROUP
+    heads = query_sets // HEAD_DIM
+    piece = quarter // CHAIN
+    vmem = pl.BlockSpec(memory_space=pltpu.VMEM)
+    dma = pltpu.SemaphoreType.DMA
+    others = GROUP - 1
+    return pl.pallas_call(
+        functools.partial(grouped_kernel, groups),
+        in_specs=[vmem] * 11,
+        out_specs=[vmem] * 2,
+        out_shape=[
+            jax.ShapeDtypeStruct((rows, width), BF16),
+            jax.ShapeDtypeStruct(query_rows.shape, BF16),
+        ],
+        scratch_shapes=[
+            pltpu.VMEM((groups, GROUP, rows, pairs), BF16),
+            pltpu.VMEM((GROUP, rows, query_sets), BF16),
+            pltpu.VMEM((GROUP, rows, query_sets), BF16),
+            pltpu.VMEM((GROUP, STATE, quarter), BF16),
+            pltpu.VMEM((GROUP, STATE, quarter), BF16),
+            pltpu.VMEM((GROUP, 8, quarter), F32),
+            pltpu.VMEM((GROUP, 8, quarter), F32),
+            pltpu.VMEM((CHAIN, STATE, piece), BF16),
+            pltpu.VMEM((CHAIN, STATE, piece), BF16),
+            pltpu.VMEM((GROUP, CHAIN, STATE, piece), BF16),
+            pltpu.VMEM((STATE, width), BF16),
+            pltpu.VMEM((rows, width), F32),
+            pltpu.VMEM((GROUP * heads, rows, HEAD_DIM), F32),
+            pltpu.VMEM((GROUP * heads, rows, HEAD_DIM), F32),
+            pltpu.VMEM((GROUP * heads, rows, HEAD_DIM), F32),
+            pltpu.VMEM((rows, 128), F32),
+            pltpu.VMEM((rows, 128), F32),
+            dma((2, others)),
+            dma((2, others)),
+            dma((others,)),
+            dma((others,)),
+            dma((others,)),
+            dma((others,)),
+            dma((others,)),
+            dma((others,)),
+            dma((groups - 1, GROUP)),
+            dma((groups - 1, GROUP)),
+            dma((CHAIN,)),
+            dma((CHAIN,)),
+            dma((CHAIN, others)),
+            dma((CHAIN, others)),
+            dma((others,)),
+            dma((others,)),
+            dma((1,)),
+            dma((1,)),
+        ],
+        compiler_params=pltpu.CompilerParams(
+            collective_id=0, has_side_effects=True, vmem_limit_bytes=50 * 2**20
+        ),
+        cost_estimate=pl.CostEstimate(
+            flops=6 * 10**9, bytes_accessed=10 * 2**20, transcendentals=12 * 10**6
+        ),
+        name="hybrid_layers",
+    )(
+        ssm_input,
+        gate_input,
+        write_proj,
+        read_proj,
+        cum_blocks,
+        cum_t,
+        jnp.repeat(skip_gain, HEAD_P)[None],
+        norm_gain[None],
+        query_rows,
+        key_rows,
+        value_rows,
+    )
+
+
 def solution(mesh):
     in_specs = (
         P("ctx", "heads"),
@@ -204,4 +727,7 @@
         P("ctx", "heads"),
     )
     out_specs = (P("ctx", "heads"), P("ctx", "heads"))
-    return jax.shard_map(body, mesh=mesh, in_specs=in_specs, out_specs=out_specs, check_vma=False)
+    ctx, heads = mesh.shape["ctx"], mesh.shape["heads"]
+    grouped = ctx % GROUP == 0 and ctx > GROUP and KV_HEADS // heads == GROUP and heads == 2
+    chosen = functools.partial(grouped_body, ctx // GROUP) if grouped else body
+    return jax.shard_map(chosen, mesh=mesh, in_specs=in_specs, out_specs=out_specs, check_vma=False)

time: 572 us -> 91.3 us (0.16); the launches traced: 564 us -> 90.9 us
  waiting for transfers between devices: 286 us -> 0 us
  matrix products: 90 us -> 0.24 us
  Pallas kernels: 0 us -> 79.9 us
  other arithmetic: 60.3 us -> 0 us
  local copies, waits for them, and re-layouts: 53.2 us -> 10 us
  blocking collectives: 36.7 us -> 0 us
  loops' own time: 22.5 us -> 0 us
  between operations: 15.1 us -> 0.69 us
    all_gather x3 -> x0, waiting for transfers between devices: 285 us -> none  [the longest x1 233 us: carried_in(): gathered = jax.tree.map(lambda a: lax.all_gather(a, axis), part)]
    dot_general x30 -> x1, matrix products: 90 us -> 0.24 us  [grouped_body(): cum = jnp.dot(causal, log_decay, precision=lax.Precision.HIGHEST)]
    pallas_call x0 -> x1, Pallas kernels: none -> 79.9 us  [grouped_body(): pl.pallas_call(functools.partial(grouped_kernel, groups), in_specs=[vmem]...]
    add x54 -> x0, other arithmetic: 38.3 us -> none  [the longest x15 29.4 us: chain_combine(): later[0][:, None, None] * earlier[1] + later[1]]
    unnamed x1 -> x0, blocking collectives: 34.2 us -> none
    reshape x8 -> x1, local copies, waits for them, and re-layouts: 26.3 us -> 0.27 us  [grouped_body(): cum_blocks = jnp.transpose(cum.reshape(rows, steps, WIDE), (1, 0, 2))]
    another operation x19 -> x0, loops' own time: 22.5 us -> none  [the longest x1 20.8 us: attention_local(): lax.scan(inner_step, carries, (key_blocks, value_blocks, offsets))]
    reduce_sum x14 -> x0, other arithmetic: 10.4 us -> none  [the longest x13 7.83 us: compute(): new_sum = rescale * running_sum + jnp.sum(weights, axis=2)]
  transfers between devices with their start and end apart: 3 -> 0, of which waited for: 2 -> 0; matrix products, arithmetic and copies ran while one was open for 26% -> 0% of each run, Pallas kernels for 0% -> 0%
where the time goes in v2:
time: 91.3 us; the launch traced here: 90.9 us
  Pallas kernels  79.9 us (88%)
  local copies, waits for them, and re-layouts  10 us (11%)
    pallas_call x1, Pallas kernels, grouped_body(): pl.pallas_call(functools.partial(grouped_kernel, groups), in_specs=[vmem]...  79.9 us
    unnamed x16, local copies, waits for them, and re-layouts  8.89 us

profile of v2, /device:TPU:24, one launch (start us, length us, event | category | flops | bytes accessed | tf_op | source)
XLA Modules:
  0.0 90.9 jit_solution(12327490341595963191)
XLA Ops:
  0.6 0.0 copy-start
  0.6 0.8 broadcast_in_dim.8
  1.4 0.1 broadcast_in_dim_reshape.3.skip_ref
  1.5 0.0 copy-done
  1.5 0.2 fusion
  1.8 0.3 copy.12
  2.0 0.0 copy-start.1
  2.0 1.1 %copy-done.1 = bf16[192,2048]{1,0:T(8,128)(2,1)S(1)} copy-done((bf16[192,2048]{1,0:T(8,128)(2,1)S(1)}, bf16[192,2048]{1,0:T(8,128)(2,1)}, u32[]{:S(2)}) %copy-start.1) | copy-done | bytes 786456
  3.2 0.0 copy-start.2
  3.2 0.9 %copy-done.2 = bf16[192,512]{1,0:T(8,128)(2,1)S(1)} copy-done((bf16[192,512]{1,0:T(8,128)(2,1)S(1)}, bf16[192,512]{1,0:T(8,128)(2,1)}, u32[]{:S(2)}) %copy-start.2) | copy-done | bytes 196632
  4.1 0.0 copy-start.3
  4.1 0.9 %copy-done.3 = bf16[192,512]{1,0:T(8,128)(2,1)S(1)} copy-done((bf16[192,512]{1,0:T(8,128)(2,1)S(1)}, bf16[192,512]{1,0:T(8,128)(2,1)}, u32[]{:S(2)}) %copy-start.3) | copy-done | bytes 196632
  5.0 0.0 copy-start.4
  5.0 0.8 copy-done.4
  5.8 0.0 copy-start.5
  5.8 0.8 copy-done.5
  6.6 0.0 copy-start.6
  6.6 0.7 copy-done.6
  7.3 79.9 %hybrid_layers.1 = (bf16[192,4096]{1,0:T(8,128)(2,1)}, bf16[192,2048]{1,0:T(8,128)(2,1)S(1)}) custom-call(bf16[192,4096]{1,0:T(8,128)(2,1)} %x_ref.1, bf16[192,4096]{1,0:T(8,128)(2,1)} %gate_ref.1, bf16[192,128]{1,0:T(8,128)(2,1)S(1)} %copy-done.4, bf16[192,128]{1,0:T(8,128)(2,1)S(1)} %copy-done.5, f32[8,192,8]{2,1,0:T(8,128)S(1)} %bitcast.7, ...), custom_call_target="tpu_custom_call" | custom-call | flops 6000000000 | bytes 10485760 | tf_op jit(solution)/shard_map/hybrid_layers/pallas_call | solution.py:649
  87.3 2.7 %copy.15 = bf16[192,4096]{1,0:T(8,128)(2,1)} copy(bf16[192,4096]{1,0:T(8,128)(2,1)} %get-tuple-element.4) | data formatting | bytes 3145728
  90.0 0.9 copy.16
Async XLA Ops:
  0.6 0.9 copy-start
  2.0 1.1 %copy-start.1 = (bf16[192,2048]{1,0:T(8,128)(2,1)S(1)}, bf16[192,2048]{1,0:T(8,128)(2,1)}, u32[]{:S(2)}) copy-start(bf16[192,2048]{1,0:T(8,128)(2,1)} %query_ref.1) | copy-start | bytes 2359300
  3.2 0.9 %copy-start.2 = (bf16[192,512]{1,0:T(8,128)(2,1)S(1)}, bf16[192,512]{1,0:T(8,128)(2,1)}, u32[]{:S(2)}) copy-start(bf16[192,512]{1,0:T(8,128)(2,1)} %key_ref.1) | copy-start | bytes 589828
  4.1 0.9 %copy-start.3 = (bf16[192,512]{1,0:T(8,128)(2,1)S(1)}, bf16[192,512]{1,0:T(8,128)(2,1)}, u32[]{:S(2)}) copy-start(bf16[192,512]{1,0:T(8,128)(2,1)} %value_ref.1) | copy-start | bytes 589828
  5.0 0.8 copy-start.4
  5.8 0.8 copy-start.5
  6.6 0.7 copy-start.6

commit v3 on v2

--- a/solution.py
+++ b/solution.py
@@ -227,8 +227,8 @@
 
 def grouped_kernel(
     groups,
-    x_ref,
-    gate_ref,
+    x_hbm,
+    gate_hbm,
     write_ref,
     read_ref,
     cum_ref,
@@ -240,6 +240,8 @@
     value_ref,
     ssm_ref,
     attn_ref,
+    x_ref,
+    gate_ref,
     kv_buf,
     q_buf,
     o_buf,
@@ -257,6 +259,7 @@
     acc_buf,
     square_own,
     square_other,
+    load_sem,
     kv_send,
     kv_recv,
     q_send,
@@ -276,8 +279,7 @@
     square_send,
     square_recv,
 ):
-    rows = x_ref.shape[0]
-    width = x_ref.shape[1]
+    rows, width = x_ref.shape
     quarter = width // GROUP
     blocks = width // BLOCK
     own = lax.axis_index("ctx")
@@ -373,6 +375,22 @@
     def square_copy():
         return remote(square_own, square_other, square_send.at[0], square_recv.at[0], heads=other)
 
+    def loads():
+        own_keys = lanes(place * key_sets, key_sets)
+        pairs = [
+            (x_hbm, x_ref),
+            (key_ref.at[:, own_keys], kv_buf.at[0, 0, :, pl.ds(0, key_sets)]),
+            (value_ref.at[:, own_keys], kv_buf.at[0, 0, :, pl.ds(key_sets, key_sets)]),
+            (query_ref.at[:, lanes(place * query_sets, query_sets)], q_buf.at[0]),
+            (gate_hbm, gate_ref),
+        ]
+        return [
+            pltpu.make_async_copy(src, dst, load_sem.at[n]) for n, (src, dst) in enumerate(pairs)
+        ]
+
+    for copy in loads():
+        copy.start()
+
     barrier = pltpu.get_barrier_semaphore()
     for j in range(1, GROUP):
         pl.semaphore_signal(
@@ -388,9 +406,9 @@
     for j in range(1, GROUP):
         for copy in kv_copies(j):
             copy.start()
-    own_columns = lanes(place * key_sets, key_sets)
-    kv_buf[0, 0, :, 0:key_sets] = key_ref[:, own_columns]
-    kv_buf[0, 0, :, key_sets:] = value_ref[:, own_columns]
+    for j in range(1, GROUP):
+        q_copy(j).start()
+    loads()[0].wait()
 
     def state_block(j, b):
         index = peer_place[j] * (quarter // BLOCK) + b
@@ -416,9 +434,6 @@
         if j > 0:
             for copy in state_copies(j):
                 copy.start()
-    for j in range(1, GROUP):
-        q_copy(j).start()
-    q_buf[0] = query_ref[:, lanes(place * query_sets, query_sets)]
 
     def forward(step):
         if step < groups - 1:
@@ -461,6 +476,8 @@
         return carry
 
     lax.fori_loop(0, blocks // 2, local_block, 0)
+    for copy in loads()[1:]:
+        copy.wait()
     for j in range(1, GROUP):
         for copy in kv_copies(j):
             copy.wait_recv()
@@ -498,55 +515,68 @@
     heads = query_sets // HEAD_DIM
     key_count = GROUP * rows
 
+    def own_blocks(count):
+        keys_values = [kv_buf[0, xor_place(place, k)] for k in range(count)]
+        return jnp.concatenate(keys_values) if count > 1 else keys_values[0]
+
+    def attend_own():
+        row = lax.broadcasted_iota(jnp.int32, (rows, 1), 0)
+        for block in range(GROUP):
+            entry = xor_place(place, block)
+            keys_values = own_blocks(block + 1)
+            keys, values = keys_values[:, :HEAD_DIM], keys_values[:, HEAD_DIM:]
+            key_total = (block + 1) * rows
+            visible = (
+                lax.broadcasted_iota(jnp.int32, (rows, key_total), 1) <= row + block * rows
+            )
+            for h in range(heads):
+                query = q_buf[entry, :, h * HEAD_DIM : (h + 1) * HEAD_DIM]
+                scores = lax.dot_general(
+                    query, keys, (((1,), (1,)), ((), ())), preferred_element_type=F32
+                )
+                scores = jnp.where(visible, scores, -1e30)
+                new_max = jnp.max(scores, axis=1, keepdims=True)
+                weights = jnp.exp2((scores - new_max) * factor)
+                total = jnp.sum(weights, axis=1, keepdims=True)
+                lane = lax.broadcasted_iota(jnp.int32, (rows, HEAD_DIM), 1)
+                at = entry * heads + h
+                top_buf[at] = jnp.broadcast_to(new_max, (rows, HEAD_DIM))
+                sum_buf[at] = jnp.where(lane == 0, total, 0.0)
+                acc_buf[at] = jnp.dot(weights.astype(BF16), values, preferred_element_type=F32)
+
     def attend(step):
-        first = step == 0
         keys = kv_buf[step, :, :, 0:HEAD_DIM].reshape(key_count, HEAD_DIM)
         values = kv_buf[step, :, :, HEAD_DIM:].reshape(key_count, HEAD_DIM)
-        if first:
-            column = lax.broadcasted_iota(jnp.int32, (1, key_count), 1)
-            shift = place * rows
-            for j in range(1, GROUP):
-                shift = jnp.where(column >= j * rows, (peer_place[j] - j) * rows, shift)
-            positions = column + shift
 
         def one(block, carry):
-            if first:
-                row = lax.broadcasted_iota(jnp.int32, (rows, 1), 0)
-                visible = positions <= row + xor_place(place, block) * rows
             for h in range(heads):
                 at = block * heads + h
                 query = q_buf[block, :, h * HEAD_DIM : (h + 1) * HEAD_DIM]
                 scores = lax.dot_general(
                     query, keys, (((1,), (1,)), ((), ())), preferred_element_type=F32
                 )
-                if first:
-                    scores = jnp.where(visible, scores, -1e30)
                 new_max = jnp.max(scores, axis=1, keepdims=True)
-                if not first:
-                    new_max = jnp.maximum(new_max, top_buf[at][:, :1])
+                new_max = jnp.maximum(new_max, top_buf[at][:, :1])
                 weights = jnp.exp2((scores - new_max) * factor)
                 new_sum = weights[:, :HEAD_DIM]
                 for k in range(1, key_count // HEAD_DIM):
                     new_sum = new_sum + weights[:, k * HEAD_DIM : (k + 1) * HEAD_DIM]
                 new_acc = jnp.dot(weights.astype(BF16), values, preferred_element_type=F32)
-                if not first:
-                    rescale = jnp.exp2((top_buf[at] - new_max) * factor)
-                    new_sum = new_sum + rescale * sum_buf[at]
-                    new_acc = new_acc + rescale * acc_buf[at]
+                rescale = jnp.exp2((top_buf[at] - new_max) * factor)
+                sum_buf[at] = new_sum + rescale * sum_buf[at]
+                acc_buf[at] = new_acc + rescale * acc_buf[at]
                 top_buf[at] = jnp.broadcast_to(new_max, (rows, HEAD_DIM))
-                sum_buf[at] = new_sum
-                acc_buf[at] = new_acc
             return carry
 
         lax.fori_loop(0, GROUP, one, 0)
 
+    for j in range(1, GROUP):
+        q_copy(j).wait_recv()
+    attend_own()
     for j in range(1, GROUP):
         for copy in state_copies(j):
             copy.wait_recv()
     pl.when(level == 0)(chain)
-    for j in range(1, GROUP):
-        q_copy(j).wait_recv()
-    attend(0)
     for step in range(1, groups):
         forward(step)
         if step < groups - 1:
@@ -644,17 +674,20 @@
     heads = query_sets // HEAD_DIM
     piece = quarter // CHAIN
     vmem = pl.BlockSpec(memory_space=pltpu.VMEM)
+    hbm = pl.BlockSpec(memory_space=pl.ANY)
     dma = pltpu.SemaphoreType.DMA
     others = GROUP - 1
     return pl.pallas_call(
         functools.partial(grouped_kernel, groups),
-        in_specs=[vmem] * 11,
+        in_specs=[hbm] * 2 + [vmem] * 6 + [hbm] * 3,
         out_specs=[vmem] * 2,
         out_shape=[
             jax.ShapeDtypeStruct((rows, width), BF16),
             jax.ShapeDtypeStruct(query_rows.shape, BF16),
         ],
         scratch_shapes=[
+            pltpu.VMEM((rows, width), BF16),
+            pltpu.VMEM((rows, width), BF16),
             pltpu.VMEM((groups, GROUP, rows, pairs), BF16),
             pltpu.VMEM((GROUP, rows, query_sets), BF16),
             pltpu.VMEM((GROUP, rows, query_sets), BF16),
@@ -672,6 +705,7 @@
             pltpu.VMEM((GROUP * heads, rows, HEAD_DIM), F32),
             pltpu.VMEM((rows, 128), F32),
             pltpu.VMEM((rows, 128), F32),
+            dma((5,)),
             dma((2, others)),
             dma((2, others)),
             dma((others,)),

time: 91.3 us -> 83.1 us (0.910)
  Pallas kernels: 79.9 us -> 71.7 us
    pallas_call x1, Pallas kernels: 79.9 us -> 71.7 us  [grouped_body(): pl.pallas_call(functools.partial(grouped_kernel, groups), in_specs=[hbm]...]
where the time goes in v3:
time: 83.1 us; the launch traced here: 82.6 us
  Pallas kernels  71.7 us (86%)
  local copies, waits for them, and re-layouts  10 us (12%)
    pallas_call x1, Pallas kernels, grouped_body(): pl.pallas_call(functools.partial(grouped_kernel, groups), in_specs=[hbm]...  71.7 us
    unnamed x16, local copies, waits for them, and re-layouts  8.89 us

profile of v3, /device:TPU:24, one launch (start us, length us, event | category | flops | bytes accessed | tf_op | source)
XLA Modules:
  0.0 82.6 jit_solution(11507256670910963382)
XLA Ops:
  0.6 0.0 copy-start
  0.6 0.8 broadcast_in_dim.8
  1.4 0.1 broadcast_in_dim_reshape.3.skip_ref
  1.5 0.0 copy-done
  1.5 0.2 fusion
  1.8 0.3 copy.12
  2.0 0.0 copy-start.1
  2.0 1.1 %copy-done.1 = bf16[192,2048]{1,0:T(8,128)(2,1)S(1)} copy-done((bf16[192,2048]{1,0:T(8,128)(2,1)S(1)}, bf16[192,2048]{1,0:T(8,128)(2,1)}, u32[]{:S(2)}) %copy-start.1) | copy-done | bytes 786456
  3.2 0.0 copy-start.2
  3.2 0.9 %copy-done.2 = bf16[192,512]{1,0:T(8,128)(2,1)S(1)} copy-done((bf16[192,512]{1,0:T(8,128)(2,1)S(1)}, bf16[192,512]{1,0:T(8,128)(2,1)}, u32[]{:S(2)}) %copy-start.2) | copy-done | bytes 196632
  4.1 0.0 copy-start.3
  4.1 0.9 %copy-done.3 = bf16[192,512]{1,0:T(8,128)(2,1)S(1)} copy-done((bf16[192,512]{1,0:T(8,128)(2,1)S(1)}, bf16[192,512]{1,0:T(8,128)(2,1)}, u32[]{:S(2)}) %copy-start.3) | copy-done | bytes 196632
  5.0 0.0 copy-start.4
  5.0 0.8 copy-done.4
  5.8 0.0 copy-start.5
  5.8 0.8 copy-done.5
  6.6 0.0 copy-start.6
  6.6 0.7 copy-done.6
  7.3 71.7 %hybrid_layers.1 = (bf16[192,4096]{1,0:T(8,128)(2,1)}, bf16[192,2048]{1,0:T(8,128)(2,1)S(1)}) custom-call(bf16[192,4096]{1,0:T(8,128)(2,1)} %x_hbm.1, bf16[192,4096]{1,0:T(8,128)(2,1)} %gate_hbm.1, bf16[192,128]{1,0:T(8,128)(2,1)S(1)} %copy-done.4, bf16[192,128]{1,0:T(8,128)(2,1)S(1)} %copy-done.5, f32[8,192,8]{2,1,0:T(8,128)S(1)} %bitcast.7, ...), custom_call_target="tpu_custom_call" | custom-call | flops 6000000000 | bytes 10485760 | tf_op jit(solution)/shard_map/hybrid_layers/pallas_call | solution.py:680
  79.0 2.7 %copy.15 = bf16[192,4096]{1,0:T(8,128)(2,1)} copy(bf16[192,4096]{1,0:T(8,128)(2,1)} %get-tuple-element.4) | data formatting | bytes 3145728
  81.7 0.9 %copy.16 = bf16[192,2048]{1,0:T(8,128)(2,1)} copy(bf16[192,2048]{1,0:T(8,128)(2,1)S(1)} %get-tuple-element.5) | data formatting | bytes 1572864
Async XLA Ops:
  0.6 0.9 %copy-start = (f32[192,64]{0,1:T(8,128)S(1)}, f32[192,64]{0,1:T(8,128)}, u32[]{:S(2)}) copy-start(f32[192,64]{0,1:T(8,128)} %param.14) | copy-start | bytes 147460
  2.0 1.1 %copy-start.1 = (bf16[192,2048]{1,0:T(8,128)(2,1)S(1)}, bf16[192,2048]{1,0:T(8,128)(2,1)}, u32[]{:S(2)}) copy-start(bf16[192,2048]{1,0:T(8,128)(2,1)} %query_ref.1) | copy-start | bytes 2359300
  3.2 0.9 %copy-start.2 = (bf16[192,512]{1,0:T(8,128)(2,1)S(1)}, bf16[192,512]{1,0:T(8,128)(2,1)}, u32[]{:S(2)}) copy-start(bf16[192,512]{1,0:T(8,128)(2,1)} %key_ref.1) | copy-start | bytes 589828
  4.1 0.9 %copy-start.3 = (bf16[192,512]{1,0:T(8,128)(2,1)S(1)}, bf16[192,512]{1,0:T(8,128)(2,1)}, u32[]{:S(2)}) copy-start(bf16[192,512]{1,0:T(8,128)(2,1)} %value_ref.1) | copy-start | bytes 589828
  5.0 0.8 copy-start.4
  5.8 0.8 copy-start.5
  6.6 0.7 copy-start.6

commit v4 on v3

--- a/solution.py
+++ b/solution.py
@@ -214,27 +214,28 @@
     return pl.ds(pl.multiple_of(start, 128), size)
 
 
-def expand_heads(per_head):
+def spread_heads(per_head):
     first = lax.broadcasted_iota(jnp.int32, (WIDE, BLOCK), 0) * HEAD_P
     column = lax.broadcasted_iota(jnp.int32, (WIDE, BLOCK), 1)
     spread = jnp.where((column >= first) & (column < first + HEAD_P), 1.0, 0.0).astype(BF16)
+    return jnp.dot(per_head.astype(BF16), spread, preferred_element_type=F32)
+
+
+def expand_heads(per_head):
     high = per_head.astype(BF16)
-    low = (per_head - high.astype(F32)).astype(BF16)
-    return jnp.dot(high, spread, preferred_element_type=F32) + jnp.dot(
-        low, spread, preferred_element_type=F32
-    )
+    return spread_heads(high) + spread_heads(per_head - high.astype(F32))
 
 
 def grouped_kernel(
     groups,
     x_hbm,
     gate_hbm,
-    write_ref,
-    read_ref,
-    cum_ref,
-    cum_t_ref,
-    skip_ref,
-    gain_ref,
+    write_hbm,
+    read_hbm,
+    cum_hbm,
+    cum_t_hbm,
+    skip_hbm,
+    gain_hbm,
     query_ref,
     key_ref,
     value_ref,
@@ -242,6 +243,12 @@
     attn_ref,
     x_ref,
     gate_ref,
+    write_ref,
+    read_ref,
+    cum_ref,
+    cum_t_ref,
+    skip_ref,
+    gain_ref,
     kv_buf,
     q_buf,
     o_buf,
@@ -379,6 +386,12 @@
         own_keys = lanes(place * key_sets, key_sets)
         pairs = [
             (x_hbm, x_ref),
+            (cum_hbm, cum_ref),
+            (write_hbm, write_ref),
+            (read_hbm, read_ref),
+            (cum_t_hbm, cum_t_ref),
+            (skip_hbm, skip_ref),
+            (gain_hbm, gain_ref),
             (key_ref.at[:, own_keys], kv_buf.at[0, 0, :, pl.ds(0, key_sets)]),
             (value_ref.at[:, own_keys], kv_buf.at[0, 0, :, pl.ds(key_sets, key_sets)]),
             (query_ref.at[:, lanes(place * query_sets, query_sets)], q_buf.at[0]),
@@ -408,26 +421,27 @@
             copy.start()
     for j in range(1, GROUP):
         q_copy(j).start()
-    loads()[0].wait()
+    for copy in loads()[:3]:
+        copy.wait()
 
     def state_block(j, b):
         index = peer_place[j] * (quarter // BLOCK) + b
         cum = cum_ref[index]
         last = cum[rows - 1 :, :]
-        weight = expand_heads(jnp.exp(last - cum))
-        scaled = (x_ref[:, lanes(index * BLOCK, BLOCK)].astype(F32) * weight).astype(BF16)
+        weight = spread_heads(jnp.exp(last - cum)).astype(BF16)
+        scaled = x_ref[:, lanes(index * BLOCK, BLOCK)] * weight
         state = lax.dot_general(
             write_ref[...], scaled, (((0,), (0,)), ((), ())), preferred_element_type=F32
         )
-        decay = expand_heads(jnp.exp(jnp.broadcast_to(last, (8, WIDE))))
         columns = slice(b * BLOCK, (b + 1) * BLOCK)
         if j == 0:
             states[0, :, columns] = state.astype(BF16)
-            decays[0, :, columns] = decay
+            decays[0, b : b + 1, 0:WIDE] = last
         else:
             own_states[j, :, columns] = state.astype(BF16)
-            own_decays[j, :, columns] = decay
-
+            own_decays[j, b : b + 1, 0:WIDE] = last
+
+    own_decays[...] = jnp.zeros(own_decays.shape, F32)
     for j in (3, 1, 2, 0):
         for b in range(quarter // BLOCK):
             state_block(j, b)
@@ -451,6 +465,9 @@
             def _():
                 for j in range(GROUP):
                     up_copy(step - 1, j).wait_recv()
+
+    for copy in loads()[3:]:
+        copy.wait()
 
     inner = lax.dot_general(
         read_ref[...], write_ref[...], (((1,), (1,)), ((), ())), preferred_element_type=F32
@@ -476,8 +493,6 @@
         return carry
 
     lax.fori_loop(0, blocks // 2, local_block, 0)
-    for copy in loads()[1:]:
-        copy.wait()
     for j in range(1, GROUP):
         for copy in kv_copies(j):
             copy.wait_recv()
@@ -485,6 +500,22 @@
     lax.fori_loop(blocks // 2, blocks, local_block, 0)
 
     def chain():
+        for j in range(1, GROUP):
+            for copy in state_copies(j):
+                copy.wait_recv()
+        passed = [
+            [
+                expand_heads(
+                    jnp.exp(
+                        jnp.broadcast_to(
+                            decays[xor_place(place, k), b : b + 1, 0:WIDE], (8, WIDE)
+                        )
+                    )
+                )[0:1, :]
+                for b in range(quarter // BLOCK)
+            ]
+            for k in range(GROUP)
+        ]
         for c in range(CHAIN):
             columns = slice(c * piece, (c + 1) * piece)
 
@@ -500,7 +531,9 @@
             for k in range(GROUP):
                 prefix[k, c] = state.astype(BF16)
                 j = xor_place(place, k)
-                state = decays[j, 0:1, columns] * state + states[j, :, columns].astype(F32)
+                at = c * piece % BLOCK
+                decay = passed[k][c * piece // BLOCK][:, at : at + piece]
+                state = decay * state + states[j, :, columns].astype(F32)
             carry_out[c] = state.astype(BF16)
 
             @pl.when(level < top)
@@ -549,23 +582,28 @@
         values = kv_buf[step, :, :, HEAD_DIM:].reshape(key_count, HEAD_DIM)
 
         def one(block, carry):
-            for h in range(heads):
-                at = block * heads + h
-                query = q_buf[block, :, h * HEAD_DIM : (h + 1) * HEAD_DIM]
-                scores = lax.dot_general(
-                    query, keys, (((1,), (1,)), ((), ())), preferred_element_type=F32
-                )
-                new_max = jnp.max(scores, axis=1, keepdims=True)
-                new_max = jnp.maximum(new_max, top_buf[at][:, :1])
-                weights = jnp.exp2((scores - new_max) * factor)
-                new_sum = weights[:, :HEAD_DIM]
-                for k in range(1, key_count // HEAD_DIM):
-                    new_sum = new_sum + weights[:, k * HEAD_DIM : (k + 1) * HEAD_DIM]
-                new_acc = jnp.dot(weights.astype(BF16), values, preferred_element_type=F32)
-                rescale = jnp.exp2((top_buf[at] - new_max) * factor)
-                sum_buf[at] = new_sum + rescale * sum_buf[at]
-                acc_buf[at] = new_acc + rescale * acc_buf[at]
-                top_buf[at] = jnp.broadcast_to(new_max, (rows, HEAD_DIM))
+            query = jnp.concatenate(
+                [q_buf[block, :, h * HEAD_DIM : (h + 1) * HEAD_DIM] for h in range(heads)]
+            )
+            at = pl.ds(block * heads, heads)
+            stacked = (heads * rows, HEAD_DIM)
+            old_max = top_buf[at].reshape(stacked)
+            scores = lax.dot_general(
+                query, keys, (((1,), (1,)), ((), ())), preferred_element_type=F32
+            )
+            new_max = jnp.maximum(jnp.max(scores, axis=1, keepdims=True), old_max[:, :1])
+            weights = jnp.exp2((scores - new_max) * factor)
+            new_sum = weights[:, :HEAD_DIM]
+            for k in range(1, key_count // HEAD_DIM):
+                new_sum = new_sum + weights[:, k * HEAD_DIM : (k + 1) * HEAD_DIM]
+            new_acc = jnp.dot(weights.astype(BF16), values, preferred_element_type=F32)
+            rescale = jnp.exp2((old_max - new_max) * factor)
+            new_sum = new_sum + rescale * sum_buf[at].reshape(stacked)
+            new_acc = new_acc + rescale * acc_buf[at].reshape(stacked)
+            shape = (heads, rows, HEAD_DIM)
+            top_buf[at] = jnp.broadcast_to(new_max, stacked).reshape(shape)
+            sum_buf[at] = new_sum.reshape(shape)
+            acc_buf[at] = new_acc.reshape(shape)
             return carry
 
         lax.fori_loop(0, GROUP, one, 0)
@@ -573,9 +611,6 @@
     for j in range(1, GROUP):
         q_copy(j).wait_recv()
     attend_own()
-    for j in range(1, GROUP):
-        for copy in state_copies(j):
-            copy.wait_recv()
     pl.when(level == 0)(chain)
     for step in range(1, groups):
         forward(step)
@@ -679,7 +714,7 @@
     others = GROUP - 1
     return pl.pallas_call(
         functools.partial(grouped_kernel, groups),
-        in_specs=[hbm] * 2 + [vmem] * 6 + [hbm] * 3,
+        in_specs=[hbm] * 11,
         out_specs=[vmem] * 2,
         out_shape=[
             jax.ShapeDtypeStruct((rows, width), BF16),
@@ -688,13 +723,19 @@
         scratch_shapes=[
             pltpu.VMEM((rows, width), BF16),
             pltpu.VMEM((rows, width), BF16),
+            pltpu.VMEM((rows, STATE), BF16),
+            pltpu.VMEM((rows, STATE), BF16),
+            pltpu.VMEM((steps, rows, WIDE), F32),
+            pltpu.VMEM((steps, WIDE, rows), F32),
+            pltpu.VMEM((1, width), F32),
+            pltpu.VMEM((1, width), F32),
             pltpu.VMEM((groups, GROUP, rows, pairs), BF16),
             pltpu.VMEM((GROUP, rows, query_sets), BF16),
             pltpu.VMEM((GROUP, rows, query_sets), BF16),
             pltpu.VMEM((GROUP, STATE, quarter), BF16),
             pltpu.VMEM((GROUP, STATE, quarter), BF16),
-            pltpu.VMEM((GROUP, 8, quarter), F32),
-            pltpu.VMEM((GROUP, 8, quarter), F32),
+            pltpu.VMEM((GROUP, 8, 128), F32),
+            pltpu.VMEM((GROUP, 8, 128), F32),
             pltpu.VMEM((CHAIN, STATE, piece), BF16),
             pltpu.VMEM((CHAIN, STATE, piece), BF16),
             pltpu.VMEM((GROUP, CHAIN, STATE, piece), BF16),
@@ -705,7 +746,7 @@
             pltpu.VMEM((GROUP * heads, rows, HEAD_DIM), F32),
             pltpu.VMEM((rows, 128), F32),
             pltpu.VMEM((rows, 128), F32),
-            dma((5,)),
+            dma((11,)),
             dma((2, others)),
             dma((2, others)),
             dma((others,)),

time: 83.1 us -> 78.3 us (0.942)
  Pallas kernels: 71.7 us -> 66.9 us
    pallas_call x1, Pallas kernels: 71.7 us -> 66.9 us  [grouped_body(): pl.pallas_call(functools.partial(grouped_kernel, groups), in_specs=[hbm]...]
where the time goes in v4:
time: 78.3 us; the launch traced here: 77.8 us
  Pallas kernels  66.9 us (85%)
  local copies, waits for them, and re-layouts  10 us (13%)
    pallas_call x1, Pallas kernels, grouped_body(): pl.pallas_call(functools.partial(grouped_kernel, groups), in_specs=[hbm]...  66.9 us
    unnamed x16, local copies, waits for them, and re-layouts  8.89 us

profile of v4, /device:TPU:24, one launch (start us, length us, event | category | flops | bytes accessed | tf_op | source)
XLA Modules:
  0.0 77.8 jit_solution(2930016974467450349)
XLA Ops:
  0.6 0.0 copy-start
  0.6 0.8 broadcast_in_dim.8
  1.4 0.1 broadcast_in_dim_reshape.3.skip_hbm
  1.5 0.0 copy-done
  1.5 0.2 fusion
  1.8 0.3 copy.12
  2.0 0.0 copy-start.1
  2.0 1.1 %copy-done.1 = bf16[192,2048]{1,0:T(8,128)(2,1)S(1)} copy-done((bf16[192,2048]{1,0:T(8,128)(2,1)S(1)}, bf16[192,2048]{1,0:T(8,128)(2,1)}, u32[]{:S(2)}) %copy-start.1) | copy-done | bytes 786456
  3.2 0.0 copy-start.2
  3.2 0.9 %copy-done.2 = bf16[192,512]{1,0:T(8,128)(2,1)S(1)} copy-done((bf16[192,512]{1,0:T(8,128)(2,1)S(1)}, bf16[192,512]{1,0:T(8,128)(2,1)}, u32[]{:S(2)}) %copy-start.2) | copy-done | bytes 196632
  4.1 0.0 copy-start.3
  4.1 0.9 %copy-done.3 = bf16[192,512]{1,0:T(8,128)(2,1)S(1)} copy-done((bf16[192,512]{1,0:T(8,128)(2,1)S(1)}, bf16[192,512]{1,0:T(8,128)(2,1)}, u32[]{:S(2)}) %copy-start.3) | copy-done | bytes 196632
  5.0 0.0 copy-start.4
  5.0 0.8 %copy-done.4 = bf16[192,128]{1,0:T(8,128)(2,1)S(1)} copy-done((bf16[192,128]{1,0:T(8,128)(2,1)S(1)}, bf16[192,128]{1,0:T(8,128)(2,1)}, u32[]{:S(2)}) %copy-start.4) | copy-done | bytes 49176
  5.8 0.0 copy-start.5
  5.8 0.8 %copy-done.5 = bf16[192,128]{1,0:T(8,128)(2,1)S(1)} copy-done((bf16[192,128]{1,0:T(8,128)(2,1)S(1)}, bf16[192,128]{1,0:T(8,128)(2,1)}, u32[]{:S(2)}) %copy-start.5) | copy-done | bytes 49176
  6.6 0.0 copy-start.6
  6.6 0.7 copy-done.6
  7.3 66.9 %hybrid_layers.1 = (bf16[192,4096]{1,0:T(8,128)(2,1)}, bf16[192,2048]{1,0:T(8,128)(2,1)S(1)}) custom-call(bf16[192,4096]{1,0:T(8,128)(2,1)} %x_hbm.1, bf16[192,4096]{1,0:T(8,128)(2,1)} %gate_hbm.1, bf16[192,128]{1,0:T(8,128)(2,1)S(1)} %copy-done.4, bf16[192,128]{1,0:T(8,128)(2,1)S(1)} %copy-done.5, f32[8,192,8]{2,1,0:T(8,128)S(1)} %bitcast.7, ...), custom_call_target="tpu_custom_call" | custom-call | flops 6000000000 | bytes 10485760 | tf_op jit(solution)/shard_map/hybrid_layers/pallas_call | solution.py:715
  74.2 2.7 %copy.15 = bf16[192,4096]{1,0:T(8,128)(2,1)} copy(bf16[192,4096]{1,0:T(8,128)(2,1)} %get-tuple-element.4) | data formatting | bytes 3145728
  76.9 0.9 %copy.16 = bf16[192,2048]{1,0:T(8,128)(2,1)} copy(bf16[192,2048]{1,0:T(8,128)(2,1)S(1)} %get-tuple-element.5) | data formatting | bytes 1572864
Async XLA Ops:
  0.6 0.9 %copy-start = (f32[192,64]{0,1:T(8,128)S(1)}, f32[192,64]{0,1:T(8,128)}, u32[]{:S(2)}) copy-start(f32[192,64]{0,1:T(8,128)} %param.14) | copy-start | bytes 147460
  2.0 1.1 %copy-start.1 = (bf16[192,2048]{1,0:T(8,128)(2,1)S(1)}, bf16[192,2048]{1,0:T(8,128)(2,1)}, u32[]{:S(2)}) copy-start(bf16[192,2048]{1,0:T(8,128)(2,1)} %query_ref.1) | copy-start | bytes 2359300
  3.2 0.9 %copy-start.2 = (bf16[192,512]{1,0:T(8,128)(2,1)S(1)}, bf16[192,512]{1,0:T(8,128)(2,1)}, u32[]{:S(2)}) copy-start(bf16[192,512]{1,0:T(8,128)(2,1)} %key_ref.1) | copy-start | bytes 589828
  4.1 0.9 %copy-start.3 = (bf16[192,512]{1,0:T(8,128)(2,1)S(1)}, bf16[192,512]{1,0:T(8,128)(2,1)}, u32[]{:S(2)}) copy-start(bf16[192,512]{1,0:T(8,128)(2,1)} %value_ref.1) | copy-start | bytes 589828
  5.0 0.8 %copy-start.4 = (bf16[192,128]{1,0:T(8,128)(2,1)S(1)}, bf16[192,128]{1,0:T(8,128)(2,1)}, u32[]{:S(2)}) copy-start(bf16[192,128]{1,0:T(8,128)(2,1)} %write_hbm.1) | copy-start | bytes 147460
  5.8 0.8 %copy-start.5 = (bf16[192,128]{1,0:T(8,128)(2,1)S(1)}, bf16[192,128]{1,0:T(8,128)(2,1)}, u32[]{:S(2)}) copy-start(bf16[192,128]{1,0:T(8,128)(2,1)} %read_hbm.1) | copy-start | bytes 147460
  6.6 0.7 copy-start.6

commit v5 on v4

--- a/solution.py
+++ b/solution.py
@@ -630,9 +630,6 @@
             o_copy(j, place).start()
     attn_ref[:, lanes(place * query_sets, query_sets)] = o_buf[0]
 
-    for c in range(CHAIN):
-        for j in range(1, GROUP):
-            prefix_copy(c, j, peer_place[j]).wait_recv()
     square_own[...] = jnp.zeros(square_own.shape, F32)
 
     def gate_block(index, carry):
@@ -649,7 +646,13 @@
         square_own[...] = total
         return carry
 
-    lax.fori_loop(0, blocks, gate_block, 0)
+    for j in range(GROUP):
+        if j > 0:
+            for c in range(CHAIN):
+                prefix_copy(c, j, peer_place[j]).wait_recv()
+        first = peer_place[j] * (quarter // BLOCK)
+        for b in range(quarter // BLOCK):
+            gate_block(first + b, 0)
     square_copy().start()
     square_copy().wait_recv()
     squares = jnp.sum(square_own[...] + square_other[...], axis=1, keepdims=True)
@@ -709,7 +712,7 @@
     heads = query_sets // HEAD_DIM
     piece = quarter // CHAIN
     vmem = pl.BlockSpec(memory_space=pltpu.VMEM)
-    hbm = pl.BlockSpec(memory_space=pl.ANY)
+    hbm = pl.BlockSpec(memory_space=pltpu.HBM)
     dma = pltpu.SemaphoreType.DMA
     others = GROUP - 1
     return pl.pallas_call(

time: 78.3 us -> 78.3 us (level)
  no operation moved by 1% of the time
where the time goes in v5:
time: 78.3 us; the launch traced here: 77.8 us
  Pallas kernels  66.9 us (85%)
  local copies, waits for them, and re-layouts  10 us (13%)
    pallas_call x1, Pallas kernels, grouped_body(): pl.pallas_call(functools.partial(grouped_kernel, groups), in_specs=[hbm]...  66.9 us
    unnamed x16, local copies, waits for them, and re-layouts  8.89 us

profile of v5, /device:TPU:24, one launch (start us, length us, event | category | flops | bytes accessed | tf_op | source)
XLA Modules:
  0.0 77.8 jit_solution(10167155599739759356)
XLA Ops:
  0.6 0.0 copy-start
  0.6 0.8 broadcast_in_dim.8
  1.4 0.1 broadcast_in_dim_reshape.3.skip_hbm
  1.5 0.0 copy-done
  1.5 0.2 fusion
  1.8 0.3 copy.12
  2.0 0.0 copy-start.1
  2.0 1.1 %copy-done.1 = bf16[192,2048]{1,0:T(8,128)(2,1)S(1)} copy-done((bf16[192,2048]{1,0:T(8,128)(2,1)S(1)}, bf16[192,2048]{1,0:T(8,128)(2,1)}, u32[]{:S(2)}) %copy-start.1) | copy-done | bytes 786456
  3.2 0.0 copy-start.2
  3.2 0.9 %copy-done.2 = bf16[192,512]{1,0:T(8,128)(2,1)S(1)} copy-done((bf16[192,512]{1,0:T(8,128)(2,1)S(1)}, bf16[192,512]{1,0:T(8,128)(2,1)}, u32[]{:S(2)}) %copy-start.2) | copy-done | bytes 196632
  4.1 0.0 copy-start.3
  4.1 0.9 %copy-done.3 = bf16[192,512]{1,0:T(8,128)(2,1)S(1)} copy-done((bf16[192,512]{1,0:T(8,128)(2,1)S(1)}, bf16[192,512]{1,0:T(8,128)(2,1)}, u32[]{:S(2)}) %copy-start.3) | copy-done | bytes 196632
  5.0 0.0 copy-start.4
  5.0 0.8 %copy-done.4 = bf16[192,128]{1,0:T(8,128)(2,1)S(1)} copy-done((bf16[192,128]{1,0:T(8,128)(2,1)S(1)}, bf16[192,128]{1,0:T(8,128)(2,1)}, u32[]{:S(2)}) %copy-start.4) | copy-done | bytes 49176
  5.8 0.0 copy-start.5
  5.8 0.8 %copy-done.5 = bf16[192,128]{1,0:T(8,128)(2,1)S(1)} copy-done((bf16[192,128]{1,0:T(8,128)(2,1)S(1)}, bf16[192,128]{1,0:T(8,128)(2,1)}, u32[]{:S(2)}) %copy-start.5) | copy-done | bytes 49176
  6.6 0.0 copy-start.6
  6.6 0.7 copy-done.6
  7.3 66.9 %hybrid_layers.1 = (bf16[192,4096]{1,0:T(8,128)(2,1)}, bf16[192,2048]{1,0:T(8,128)(2,1)S(1)}) custom-call(bf16[192,4096]{1,0:T(8,128)(2,1)} %x_hbm.1, bf16[192,4096]{1,0:T(8,128)(2,1)} %gate_hbm.1, bf16[192,128]{1,0:T(8,128)(2,1)S(1)} %copy-done.4, bf16[192,128]{1,0:T(8,128)(2,1)S(1)} %copy-done.5, f32[8,192,8]{2,1,0:T(8,128)S(1)} %bitcast.7, ...), custom_call_target="tpu_custom_call" | custom-call | flops 6000000000 | bytes 10485760 | tf_op jit(solution)/shard_map/hybrid_layers/pallas_call | solution.py:718
  74.3 2.7 %copy.15 = bf16[192,4096]{1,0:T(8,128)(2,1)} copy(bf16[192,4096]{1,0:T(8,128)(2,1)} %get-tuple-element.4) | data formatting | bytes 3145728
  77.0 0.9 %copy.16 = bf16[192,2048]{1,0:T(8,128)(2,1)} copy(bf16[192,2048]{1,0:T(8,128)(2,1)S(1)} %get-tuple-element.5) | data formatting | bytes 1572864
Async XLA Ops:
  0.6 0.9 %copy-start = (f32[192,64]{0,1:T(8,128)S(1)}, f32[192,64]{0,1:T(8,128)}, u32[]{:S(2)}) copy-start(f32[192,64]{0,1:T(8,128)} %param.14) | copy-start | bytes 147460
  2.0 1.1 %copy-start.1 = (bf16[192,2048]{1,0:T(8,128)(2,1)S(1)}, bf16[192,2048]{1,0:T(8,128)(2,1)}, u32[]{:S(2)}) copy-start(bf16[192,2048]{1,0:T(8,128)(2,1)} %query_ref.1) | copy-start | bytes 2359300
  3.2 0.9 %copy-start.2 = (bf16[192,512]{1,0:T(8,128)(2,1)S(1)}, bf16[192,512]{1,0:T(8,128)(2,1)}, u32[]{:S(2)}) copy-start(bf16[192,512]{1,0:T(8,128)(2,1)} %key_ref.1) | copy-start | bytes 589828
  4.1 0.9 %copy-start.3 = (bf16[192,512]{1,0:T(8,128)(2,1)S(1)}, bf16[192,512]{1,0:T(8,128)(2,1)}, u32[]{:S(2)}) copy-start(bf16[192,512]{1,0:T(8,128)(2,1)} %value_ref.1) | copy-start | bytes 589828
  5.0 0.8 %copy-start.4 = (bf16[192,128]{1,0:T(8,128)(2,1)S(1)}, bf16[192,128]{1,0:T(8,128)(2,1)}, u32[]{:S(2)}) copy-start(bf16[192,128]{1,0:T(8,128)(2,1)} %write_hbm.1) | copy-start | bytes 147460
  5.8 0.8 %copy-start.5 = (bf16[192,128]{1,0:T(8,128)(2,1)S(1)}, bf16[192,128]{1,0:T(8,128)(2,1)}, u32[]{:S(2)}) copy-start(bf16[192,128]{1,0:T(8,128)(2,1)} %read_hbm.1) | copy-start | bytes 147460
  6.6 0.7 copy-start.6
